TPU v7x, 32 devices: a whole 2x2x4 slice. The times are simulated.
32 devices in a mesh: cells: 4 (over y, x), wall: 8 (over z, core).
Axes of the slice: x: 2, y: 2, z: 4, core: 2. Of those that a mesh axis runs over, the one named last changes fastest.
Arguments:
- shape_coef: bfloat16 [3, 289, 8192], P(None, None, ('cells', 'wall')), may hold values from -3 to 3
- force_coef: bfloat16 [3, 289, 8192], P(None, None, ('cells', 'wall')), may hold values from -1.5 to 1.5
- near_cell: int32 [2048], P(('cells', 'wall')), may hold values from 0 to 255
- near_dest: int32 [2048], P(('cells', 'wall')), may hold values from 0 to 7, as said below
- near_slot: int32 [2048], P(('cells', 'wall')), may hold values from 0 to 1
- panel_centers: float32 [64, 384], P(('cells', 'wall')), may hold values from -2 to 2
- near_blocks: bfloat16 [64, 2, 384, 384], P(('cells', 'wall')), may hold values from -0.15625 to 0.15625
- near_pick: int32 [64], P(('cells', 'wall')), may hold values from 0 to 1
- src_basis: float32 [64, 384, 16], P(('cells', 'wall')), may hold values from -0.3125 to 0.3125
- far_couple: float32 [64, 8, 16, 16], P(('cells', 'wall')), may hold values from -0.5 to 0.5
- far_src: int32 [64, 8], P(('cells', 'wall')), may hold values from 0 to 63
- far_rank: int32 [64, 8], P(('cells', 'wall')), may hold values from 1 to 16
- tgt_basis: float32 [64, 16, 384], P(('cells', 'wall')), may hold values from -1.5 to 1.5
- cluster_slot: int32 [64], replicated, may hold values from 0 to 63, each once
Outputs:
- surface: bfloat16 [3, 578, 8192], P(None, None, ('cells', 'wall'))
- density: float32 [64, 384], P(('cells', 'wall'))
Inputs may be any that keep to these rules, and one draw needn't show every extreme that they name: `near_cell`: A cell of the row's own device block of 256 cells; each device holds 64 rows. `near_dest`: among the 64 rows of one device no value appears more than 16 times; in each group of 8 devices along the wall axis some value appears exactly 16 times among the rows of every device of the group. `cluster_slot`: each of 0 to 63 appears once.
All inputs are finite; a program needn't handle non-finite values.
Results may differ from a plain program's by a relative error of at most 0.0062.
Values may be sent and summed in bfloat16 or wider, within the bound.
A program may use at most 64 MiB of HBM per device.

v0:
```python
import math

import jax
import jax.numpy as jnp
import numpy as np
from jax import lax
from jax.sharding import PartitionSpec as P

ORDER = 16
ITERS = 2


soft_core = 0.25
stokes_scale = 1.0 / (8.0 * math.pi)


def shifted(array, axis, by):
    devices = lax.axis_size(axis)
    return lax.ppermute(array, axis, [(i, (i + by) % devices) for i in range(devices)])


def harmonics(order):
    lat_count = order + 1
    polar_angle = np.pi * (np.arange(lat_count) + 0.5) / lat_count
    azimuth = np.pi * np.arange(2 * lat_count) / lat_count
    cos_polar = np.repeat(np.cos(polar_angle), 2 * lat_count)
    sin_polar = np.repeat(np.sin(polar_angle), 2 * lat_count)
    az_grid = np.tile(azimuth, lat_count)
    legendre = {}
    legendre[0, 0] = cos_polar * 0.0 + 0.5 / np.sqrt(np.pi)
    for m in range(1, order + 1):
        legendre[m, m] = -np.sqrt((2.0 * m + 1.0) / (2.0 * m)) * sin_polar * legendre[m - 1, m - 1]
    for m in range(order):
        legendre[m + 1, m] = np.sqrt(2.0 * m + 3.0) * cos_polar * legendre[m, m]
    for m in range(order + 1):
        for l in range(m + 2, order + 1):
            factor = np.sqrt((4.0 * l * l - 1.0) / (l * l - m * m))
            backward = np.sqrt(((l - 1.0) ** 2 - m * m) / (4.0 * (l - 1.0) ** 2 - 1.0))
            legendre[l, m] = factor * (
                cos_polar * legendre[l - 1, m] - backward * legendre[l - 2, m]
            )
    columns = []
    for l in range(order + 1):
        for m in range(-l, l + 1):
            if m > 0:
                columns.append(np.sqrt(2.0) * legendre[l, m] * np.cos(m * az_grid))
            elif m < 0:
                columns.append(np.sqrt(2.0) * legendre[l, -m] * np.sin(-m * az_grid))
            else:
                columns.append(legendre[l, 0])
    return np.stack(columns, axis=1)


def kernel_block(pieces):
    points, forces, centers = pieces
    panels = centers.shape[1] // 3
    source = points.astype(jnp.float32)
    strength = forces.astype(jnp.float32)
    spots = centers.reshape(centers.shape[0], 3, panels)
    offset = [spots[:, a, :, None] - source[:, a, None, :] for a in range(3)]
    radius_sq = offset[0] * offset[0] + offset[1] * offset[1] + offset[2] * offset[2] + soft_core
    inverse = lax.rsqrt(radius_sq)
    inverse_cube = inverse * inverse * inverse
    along = (
        offset[0] * strength[:, 0, None, :]
        + offset[1] * strength[:, 1, None, :]
        + offset[2] * strength[:, 2, None, :]
    )
    parts = [
        jnp.sum(strength[:, a, None, :] * inverse + offset[a] * along * inverse_cube, axis=2)
        for a in range(3)
    ]
    return jnp.stack(parts, axis=1).reshape(centers.shape[0], 3 * panels) * stokes_scale


def stokes_rows(points, forces, centers, block):
    total = points.shape[0]
    width = math.gcd(total, block)
    groups = total // width
    result = lax.map(
        kernel_block,
        (
            points.reshape(groups, width, 3, points.shape[2]),
            forces.reshape(groups, width, 3, forces.shape[2]),
            centers.reshape(groups, width, centers.shape[1]),
        ),
    )
    return result.reshape(total, centers.shape[1])


def local(
    shape_coef,
    force_coef,
    near_cell,
    near_dest,
    near_slot,
    panel_centers,
    near_blocks,
    near_pick,
    src_basis,
    far_couple,
    far_src,
    far_rank,
    tgt_basis,
    cluster_slot,
):
    walls = lax.axis_size("wall")
    near_count = near_cell.shape[0]
    cluster_count = panel_centers.shape[0]
    cap = max(2, 2 * near_count // walls)
    harmonic = jnp.asarray(harmonics(ORDER), jnp.float32).astype(jnp.bfloat16)
    surface = jnp.einsum(
        "qs,asc->aqc", harmonic, shape_coef, preferred_element_type=jnp.float32
    ).astype(jnp.bfloat16)
    points = jnp.transpose(jnp.take(surface, near_cell, axis=2), (2, 0, 1))
    picked = jnp.take(force_coef, near_cell, axis=2)
    forces = jnp.einsum("qs,asn->naq", harmonic, picked, preferred_element_type=jnp.float32).astype(
        jnp.bfloat16
    )
    dest_hits = (near_dest[:, None] == jnp.arange(walls, dtype=jnp.int32)[None, :]).astype(
        jnp.int32
    )
    position = jnp.sum(jnp.cumsum(dest_hits, axis=0) * dest_hits, axis=1) - 1
    slot_index = near_dest * cap + position
    id_buffer = (
        jnp.full((walls * cap,), -1, jnp.int32).at[slot_index].set(near_slot).reshape(walls, cap)
    )
    group_centers = lax.all_gather(panel_centers, "wall", axis=0, tiled=True)
    centers = jnp.take(group_centers, near_dest * cluster_count + near_slot, axis=0)
    velocity = stokes_rows(points, forces, centers, 8)
    vel_buffer = (
        jnp.zeros((walls * cap, centers.shape[1]), jnp.float32).at[slot_index].set(velocity)
    )
    vel_buffer = vel_buffer.reshape(walls, cap, centers.shape[1])
    recv_vel, recv_ids = (
        lax.all_to_all(vel_buffer, "wall", split_axis=0, concat_axis=0, tiled=True),
        lax.all_to_all(id_buffer, "wall", split_axis=0, concat_axis=0, tiled=True),
    )
    owner_hits = (
        recv_ids[:, :, None] == jnp.arange(cluster_count, dtype=jnp.int32)[None, None, :]
    ).astype(jnp.float32)
    wall_rhs = -jnp.einsum("wkc,wkp->cp", owner_hits, recv_vel, precision=lax.Precision.HIGHEST)
    source_rows = jnp.take(cluster_slot, far_src, axis=0)
    rank_size = far_couple.shape[2]
    levels = jnp.arange(rank_size, dtype=jnp.int32)
    rank_keep = (levels[None, None, :, None] < far_rank[:, :, None, None]) & (
        levels[None, None, None, :] < far_rank[:, :, None, None]
    )
    masked = jnp.where(rank_keep, far_couple, jnp.zeros_like(far_couple))
    density = wall_rhs
    for step in range(ITERS):
        density_low = density.astype(jnp.bfloat16)
        neighbor = shifted(density_low, "wall", 1)
        paired = jnp.stack([density_low, jnp.take(neighbor, near_pick, axis=0)], axis=1)
        near_term = jnp.einsum(
            "cbij,cbj->ci", near_blocks, paired, preferred_element_type=jnp.float32
        )
        coefficients = jnp.einsum("cpr,cp->cr", src_basis, density, precision=lax.Precision.HIGHEST)
        coef_table = lax.all_gather(coefficients, ("cells", "wall"), axis=0, tiled=True)
        gathered = jnp.take(coef_table, source_rows, axis=0)
        mixed_rank = jnp.einsum("cbij,cbj->ci", masked, gathered, precision=lax.Precision.HIGHEST)
        far_term = jnp.einsum("cr,crp->cp", mixed_rank, tgt_basis, precision=lax.Precision.HIGHEST)
        density = wall_rhs - near_term - far_term
    return (surface, density)


def solution(mesh):
    return jax.shard_map(
        local,
        mesh=mesh,
        in_specs=(
            P(None, None, ("cells", "wall")),
            P(None, None, ("cells", "wall")),
            P(("cells", "wall")),
            P(("cells", "wall")),
            P(("cells", "wall")),
            P(("cells", "wall"), None),
            P(("cells", "wall"), None, None, None),
            P(("cells", "wall")),
            P(("cells", "wall"), None, None),
            P(("cells", "wall"), None, None, None),
            P(("cells", "wall"), None),
            P(("cells", "wall"), None),
            P(("cells", "wall"), None, None),
            P(),
        ),
        out_specs=(P(None, None, ("cells", "wall")), P(("cells", "wall"), None)),
        check_vma=False,
    )
```

profile of v0, /device:TPU:0, one launch (start us, length us, event | category | flops | bytes accessed | tf_op | source)
XLA Modules:
  0.0 178.8 jit_solution(9085875817535895054)
XLA Ops:
  0.6 0.8 fusion.30
  1.6 0.8 select_reduce_fusion
  2.4 0.7 compare_select_fusion.5
  3.1 0.9 scatter_custom_fusion
  4.0 0.7 all_to_all.9
  4.7 6.3 %all-to-all-start = ((s32[8,1,16]{2,1,0:T(1,128)}), s32[8,1,16]{2,1,0:T(1,128)S(1)}, u32[]{:S(2)}, u32[]{:S(2)}) async-start(s32[8,1,16]{2,1,0:T(1,128)} %bitcast.20), calls=%async_computation | async-start | bytes 8192 | tf_op jit(solution)/shard_map/all_to_all | solution.py:137
  11.0 0.7 compare_select_fusion.4
  11.6 0.7 compare_and_fusion.3
  12.3 0.7 compare_and_fusion.2
  13.0 1.8 fusion.17
  14.8 1.5 copy.36
  16.3 2.1 %copy.34 = bf16[3,289,256]{1,0,2:T(4,128)(2,1)} copy(bf16[3,289,256]{2,1,0:T(8,128)(2,1)} %param.22) | data formatting | bytes 887808 | tf_op args[1]
  18.4 0.9 gather_fusion.2
  19.3 1.9 %gather_fusion = bf16[64,3,289]{2,1,0:T(4,128)(2,1)S(1)} fusion(bf16[3,289,256]{1,0,2:T(4,128)(2,1)} %copy.34, s32[1024]{0:T(1024)S(1)} %pad_clamp_fusion.4), kind=kCustom, calls=%fused_computation.4 | custom fusion | bytes 222208 | tf_op jit(solution)/shard_map/jit(_take)/gather | solution.py:116
  22.0 14.4 %all-gather = f32[8,2,384]{2,1,0:T(2,128)S(1)} all-gather(f32[1,2,384]{2,1,0:T(2,128)S(1)} %bitcast.163), channel_id=1, replica_groups=mesh['cells'=4,'wall'=8] {'wall'}, dimensions={0}, use_global_device_ids=true | all-gather | bytes 27648 | tf_op jit(solution)/shard_map/all_gather | solution.py:128
  36.6 0.7 gather_fusion.1
  37.3 44.2 %while.10 = (s32[]{:T(128)}, f32[8,8,384]{2,1,0:T(8,128)S(1)}, bf16[8,8,3,578]{3,1,0,2:T(8,128)(2,1)S(1)}, f32[8,8,384]{2,1,0:T(8,128)S(1)}, bf16[8,8,3,578]{3,2,1,0:T(4,128)(2,1)S(1)}, /*index=5*/s32[]{:T(128)}) while((s32[]{:T(128)}, f32[8,8,384]{2,1,0:T(8,128)S(1)}, bf16[8,8,3,578]{3,1,0,2:T(8,128)(2,1)S(1)}, f32[8,8,384]{2,1,0:T(8,128)S(1)}, ...), condition=%wide.region_7.8_spmd, body=%wide.region_3.7_spmd.sunk | while | flops 18381920 | bytes 819733 | solution.py:80
  38.2 4.6 %fusion.68 = (f32[8,128]{1,0:T(8,128)S(1)}, f32[8,128]{1,0:T(8,128)S(1)}, f32[8,128]{1,0:T(8,128)S(1)}) fusion(f32[8,578]{0,1:T(8,128)S(1)} %get-tuple-element.128, f32[8,578]{0,1:T(8,128)S(1)} %get-tuple-element.129, f32[8,578]{0,1:T(8,128)S(1)} %get-tuple-element.130, f32[8,128]{1,0:T(8,128)S(1)} %get-tuple-element.131, ...), kind=kLoop, calls=%fused_computation.28.clone.1 | loop fusion | flops 18344960 | bytes 135552 | tf_op jit(solution)/shard_map/while/body/eval_jaxpr/reduce_sum | solution.py:70
  43.8 4.6 %fusion.68 = (f32[8,128]{1,0:T(8,128)S(1)}, f32[8,128]{1,0:T(8,128)S(1)}, f32[8,128]{1,0:T(8,128)S(1)}) fusion(f32[8,578]{0,1:T(8,128)S(1)} %get-tuple-element.128, f32[8,578]{0,1:T(8,128)S(1)} %get-tuple-element.129, f32[8,578]{0,1:T(8,128)S(1)} %get-tuple-element.130, f32[8,128]{1,0:T(8,128)S(1)} %get-tuple-element.131, ...), kind=kLoop, calls=%fused_computation.28.clone.1 | loop fusion | flops 18344960 | bytes 135552 | tf_op jit(solution)/shard_map/while/body/eval_jaxpr/reduce_sum | solution.py:70
  49.3 4.6 %fusion.68 = (f32[8,128]{1,0:T(8,128)S(1)}, f32[8,128]{1,0:T(8,128)S(1)}, f32[8,128]{1,0:T(8,128)S(1)}) fusion(f32[8,578]{0,1:T(8,128)S(1)} %get-tuple-element.128, f32[8,578]{0,1:T(8,128)S(1)} %get-tuple-element.129, f32[8,578]{0,1:T(8,128)S(1)} %get-tuple-element.130, f32[8,128]{1,0:T(8,128)S(1)} %get-tuple-element.131, ...), kind=kLoop, calls=%fused_computation.28.clone.1 | loop fusion | flops 18344960 | bytes 135552 | tf_op jit(solution)/shard_map/while/body/eval_jaxpr/reduce_sum | solution.py:70
  54.8 4.6 %fusion.68 = (f32[8,128]{1,0:T(8,128)S(1)}, f32[8,128]{1,0:T(8,128)S(1)}, f32[8,128]{1,0:T(8,128)S(1)}) fusion(f32[8,578]{0,1:T(8,128)S(1)} %get-tuple-element.128, f32[8,578]{0,1:T(8,128)S(1)} %get-tuple-element.129, f32[8,578]{0,1:T(8,128)S(1)} %get-tuple-element.130, f32[8,128]{1,0:T(8,128)S(1)} %get-tuple-element.131, ...), kind=kLoop, calls=%fused_computation.28.clone.1 | loop fusion | flops 18344960 | bytes 135552 | tf_op jit(solution)/shard_map/while/body/eval_jaxpr/reduce_sum | solution.py:70
  60.3 4.6 %fusion.68 = (f32[8,128]{1,0:T(8,128)S(1)}, f32[8,128]{1,0:T(8,128)S(1)}, f32[8,128]{1,0:T(8,128)S(1)}) fusion(f32[8,578]{0,1:T(8,128)S(1)} %get-tuple-element.128, f32[8,578]{0,1:T(8,128)S(1)} %get-tuple-element.129, f32[8,578]{0,1:T(8,128)S(1)} %get-tuple-element.130, f32[8,128]{1,0:T(8,128)S(1)} %get-tuple-element.131, ...), kind=kLoop, calls=%fused_computation.28.clone.1 | loop fusion | flops 18344960 | bytes 135552 | tf_op jit(solution)/shard_map/while/body/eval_jaxpr/reduce_sum | solution.py:70
  65.9 4.6 %fusion.68 = (f32[8,128]{1,0:T(8,128)S(1)}, f32[8,128]{1,0:T(8,128)S(1)}, f32[8,128]{1,0:T(8,128)S(1)}) fusion(f32[8,578]{0,1:T(8,128)S(1)} %get-tuple-element.128, f32[8,578]{0,1:T(8,128)S(1)} %get-tuple-element.129, f32[8,578]{0,1:T(8,128)S(1)} %get-tuple-element.130, f32[8,128]{1,0:T(8,128)S(1)} %get-tuple-element.131, ...), kind=kLoop, calls=%fused_computation.28.clone.1 | loop fusion | flops 18344960 | bytes 135552 | tf_op jit(solution)/shard_map/while/body/eval_jaxpr/reduce_sum | solution.py:70
  71.4 4.6 %fusion.68 = (f32[8,128]{1,0:T(8,128)S(1)}, f32[8,128]{1,0:T(8,128)S(1)}, f32[8,128]{1,0:T(8,128)S(1)}) fusion(f32[8,578]{0,1:T(8,128)S(1)} %get-tuple-element.128, f32[8,578]{0,1:T(8,128)S(1)} %get-tuple-element.129, f32[8,578]{0,1:T(8,128)S(1)} %get-tuple-element.130, f32[8,128]{1,0:T(8,128)S(1)} %get-tuple-element.131, ...), kind=kLoop, calls=%fused_computation.28.clone.1 | loop fusion | flops 18344960 | bytes 135552 | tf_op jit(solution)/shard_map/while/body/eval_jaxpr/reduce_sum | solution.py:70
  76.9 4.6 %fusion.68 = (f32[8,128]{1,0:T(8,128)S(1)}, f32[8,128]{1,0:T(8,128)S(1)}, f32[8,128]{1,0:T(8,128)S(1)}) fusion(f32[8,578]{0,1:T(8,128)S(1)} %get-tuple-element.128, f32[8,578]{0,1:T(8,128)S(1)} %get-tuple-element.129, f32[8,578]{0,1:T(8,128)S(1)} %get-tuple-element.130, f32[8,128]{1,0:T(8,128)S(1)} %get-tuple-element.131, ...), kind=kLoop, calls=%fused_computation.28.clone.1 | loop fusion | flops 18344960 | bytes 135552 | tf_op jit(solution)/shard_map/while/body/eval_jaxpr/reduce_sum | solution.py:70
  81.7 0.7 gather_fusion.3
  82.5 1.4 scatter_custom_fusion.1
  84.0 4.4 %all-to-all-start.1 = ((f32[8,16,384]{2,1,0:T(8,128)}), f32[8,16,384]{2,1,0:T(8,128)S(1)}, u32[]{:S(2)}, u32[]{:S(2)}) async-start(f32[8,16,384]{2,1,0:T(8,128)} %bitcast.29), calls=%async_computation.1 | async-start | bytes 393216 | tf_op jit(solution)/shard_map/all_to_all | solution.py:136
  88.6 8.2 %all-to-all-done.1 = f32[8,16,384]{2,1,0:T(8,128)S(1)} async-done(((f32[8,16,384]{2,1,0:T(8,128)}), f32[8,16,384]{2,1,0:T(8,128)S(1)}, u32[]{:S(2)}, u32[]{:S(2)}) %all-to-all-start.1) | async-done | bytes 196640 | tf_op jit(solution)/shard_map/all_to_all | solution.py:136
  97.2 39.5 %all-gather.1 = f32[32,2,16]{2,1,0:T(2,128)S(1)} all-gather(f32[1,2,16]{2,1,0:T(2,128)S(1)} %bitcast.162), channel_id=1, replica_groups=mesh['cells'=4,'wall'=8] {'cells','wall'}, dimensions={0}, use_global_device_ids=true | all-gather | bytes 4224 | tf_op jit(solution)/shard_map/all_gather | solution.py:159
  139.5 36.4 %all-gather.2 = f32[32,2,16]{2,1,0:T(2,128)S(1)} all-gather(f32[1,2,16]{2,1,0:T(2,128)S(1)} %bitcast.161), channel_id=1, replica_groups=mesh['cells'=4,'wall'=8] {'cells','wall'}, dimensions={0}, use_global_device_ids=true | all-gather | bytes 4224 | tf_op jit(solution)/shard_map/all_gather | solution.py:159
  178.2 0.6 bitcast_subtract_fusion
  (148 shorter events, 13.5 us)
Async XLA Ops:
  0.6 138.0 %copy-start = (bf16[2,2,384,384]{3,2,1,0:T(8,128)(2,1)S(1)}, bf16[2,2,384,384]{3,2,1,0:T(8,128)(2,1)}, u32[]{:S(2)}) copy-start(bf16[2,2,384,384]{3,2,1,0:T(8,128)(2,1)} %param.27) | copy-start | bytes 3538948
  4.7 79.3 %all-to-all-start = ((s32[8,1,16]{2,1,0:T(1,128)}), s32[8,1,16]{2,1,0:T(1,128)S(1)}, u32[]{:S(2)}, u32[]{:S(2)}) async-start(s32[8,1,16]{2,1,0:T(1,128)} %bitcast.20), calls=%async_computation | async-start | bytes 8192 | tf_op jit(solution)/shard_map/all_to_all | solution.py:137
  14.8 1.5 copy-start.2
  18.4 3.2 %copy-start.3 = (bf16[578,289,1]{0,1,2:T(8,128)(2,1)S(1)}, bf16[578,289,1]{0,1,2:T(8,128)(2,1)}, u32[]{:S(2)}) copy-start(bf16[578,289,1]{0,1,2:T(8,128)(2,1)} %constant.127) | copy-start | bytes 1002256
  19.3 2.7 %copy-start.7 = (f32[2,384]{1,0:T(2,128)S(1)}, f32[2,384]{1,0:T(2,128)}, u32[]{:S(2)}) copy-start(f32[2,384]{1,0:T(2,128)} %param.26) | copy-start | bytes 9220
  37.3 44.3 %copy-start.10 = (s32[2]{0:T(128)S(1)}, s32[2]{0:T(128)}, u32[]{:S(2)}) copy-start(s32[2]{0:T(128)} %param.28) | copy-start | bytes 28
  37.3 44.3 %copy-start.6 = (s32[2,8]{1,0:T(2,128)S(1)}, s32[2,8]{1,0:T(2,128)}, u32[]{:S(2)}) copy-start(s32[2,8]{1,0:T(2,128)} %param.31) | copy-start | bytes 196
  37.3 44.4 %copy-start.1 = (s32[64]{0:T(128)S(1)}, s32[64]{0:T(128)}, u32[]{:S(2)}) copy-start(s32[64]{0:T(128)} %param.34) | copy-start | bytes 772
  81.6 6.9 %copy-start.8 = (s32[2,8]{1,0:T(2,128)S(1)}, s32[2,8]{1,0:T(2,128)}, u32[]{:S(2)}) copy-start(s32[2,8]{1,0:T(2,128)} %param.32) | copy-start | bytes 196
  81.6 15.5 %copy-start.4 = (f32[2,384,16]{1,2,0:T(8,128)S(1)}, f32[2,384,16]{1,2,0:T(8,128)}, u32[]{:S(2)}) copy-start(f32[2,384,16]{1,2,0:T(8,128)} %param.29) | copy-start | bytes 147460
  81.6 55.8 %copy-start.9 = (f32[2,8,16,16]{3,2,1,0:T(8,128)S(1)}, f32[2,8,16,16]{3,2,1,0:T(8,128)}, u32[]{:S(2)}) copy-start(f32[2,8,16,16]{3,2,1,0:T(8,128)} %param.30) | copy-start | bytes 49156
  81.6 56.2 %copy-start.5 = (f32[2,16,384]{2,1,0:T(8,128)S(1)}, f32[2,16,384]{2,1,0:T(8,128)}, u32[]{:S(2)}) copy-start(f32[2,16,384]{2,1,0:T(8,128)} %param.33) | copy-start | bytes 147460
  84.0 12.8 %all-to-all-start.1 = ((f32[8,16,384]{2,1,0:T(8,128)}), f32[8,16,384]{2,1,0:T(8,128)S(1)}, u32[]{:S(2)}, u32[]{:S(2)}) async-start(f32[8,16,384]{2,1,0:T(8,128)} %bitcast.29), calls=%async_computation.1 | async-start | bytes 393216 | tf_op jit(solution)/shard_map/all_to_all | solution.py:136
  97.0 40.9 %collective-permute-start = (bf16[2,384]{1,0:T(2,128)(2,1)S(1)}, bf16[2,384]{1,0:T(2,128)(2,1)S(1)}, u32[]{:S(2)}, u32[]{:S(2)}) collective-permute-start(bf16[2,384]{1,0:T(2,128)(2,1)S(1)} %get-tuple-element.83), channel_id=1, source_target_pairs={{0,1},{1,2},{2,3},{3,4},{4,5},{5,6},{6,7},{7,0},{8,9},{9,10},{10,1... | collective-permute-start | bytes 4616 | tf_op jit(solution)/shard_map/ppermute | solution.py:19
  139.0 38.1 %collective-permute-start.1 = (bf16[2,384]{1,0:T(2,128)(2,1)S(1)}, bf16[2,384]{1,0:T(2,128)(2,1)S(1)}, u32[]{:S(2)}, u32[]{:S(2)}) collective-permute-start(bf16[2,384]{1,0:T(2,128)(2,1)S(1)} %get-tuple-element.65), channel_id=1, source_target_pairs={{0,1},{1,2},{2,3},{3,4},{4,5},{5,6},{6,7},{7,0},{8,9},{9,10},{10,1... | collective-permute-start | bytes 4616 | tf_op jit(solution)/shard_map/ppermute | solution.py:19
where the time goes:
time: 179 us
  blocking collectives  90.4 us (51%)
  other arithmetic  43.9 us (25%)
  local copies, waits for them, and re-layouts  19 us (11%)
  starting transfers between devices  11.2 us (6%)
  waiting for transfers between devices  8.18 us (5%)
  matrix products  4.49 us (3%)
    all_gather x2, blocking collectives, local(): lax.all_gather(coefficients, ('cells', 'wall'), axis=0, tiled=True)  75.9 us
    reduce_sum x8, other arithmetic, kernel_block(): jnp.sum(strength[:, a, None, :] * inverse + offset[a] * along * inverse_c...  36.8 us
    all_gather x1, blocking collectives, local(): group_centers = lax.all_gather(panel_centers, 'wall', axis=0, tiled=True)  14.4 us
    all_to_all x1, waiting for transfers between devices, local(): lax.all_to_all(vel_buffer, 'wall', split_axis=0, concat_axis=0, tiled=True)  8.16 us
    all_to_all x1, starting transfers between devices, local(): lax.all_to_all(id_buffer, 'wall', split_axis=0, concat_axis=0, tiled=True)  6.33 us
    dynamic_slice x32, local copies, waits for them, and re-layouts, stokes_rows(): lax.map(kernel_block, (points.reshape(groups, width, 3, points.shape[2]),...  4.48 us
    all_to_all x1, starting transfers between devices, local(): lax.all_to_all(vel_buffer, 'wall', split_axis=0, concat_axis=0, tiled=True)  4.44 us
  transfers between devices with their start and end apart: 4, of which 1 were waited for; matrix products, arithmetic and copies ran while one was open for 34% of the time, Pallas kernels for 0%

commit v1 on v0

v1 whole, which is shorter than its diff:
```python
import functools
import math

import jax
import jax.numpy as jnp
import numpy as np
from jax import lax
from jax.experimental import pallas as pl
from jax.experimental.pallas import tpu as pltpu
from jax.sharding import PartitionSpec as P

ORDER = 16
ITERS = 2
LANES = 128
ROWS = 16

soft_core = 0.25
stokes_scale = 1.0 / (8.0 * math.pi)

MESH = pl.DeviceIdType.MESH
HIGHEST = lax.Precision.HIGHEST
F32 = jnp.float32
BF16 = jnp.bfloat16
NT = (((1,), (1,)), ((), ()))


def harmonics(order):
    lat_count = order + 1
    polar_angle = np.pi * (np.arange(lat_count) + 0.5) / lat_count
    azimuth = np.pi * np.arange(2 * lat_count) / lat_count
    cos_polar = np.repeat(np.cos(polar_angle), 2 * lat_count)
    sin_polar = np.repeat(np.sin(polar_angle), 2 * lat_count)
    az_grid = np.tile(azimuth, lat_count)
    legendre = {}
    legendre[0, 0] = cos_polar * 0.0 + 0.5 / np.sqrt(np.pi)
    for m in range(1, order + 1):
        legendre[m, m] = -np.sqrt((2.0 * m + 1.0) / (2.0 * m)) * sin_polar * legendre[m - 1, m - 1]
    for m in range(order):
        legendre[m + 1, m] = np.sqrt(2.0 * m + 3.0) * cos_polar * legendre[m, m]
    for m in range(order + 1):
        for l in range(m + 2, order + 1):
            factor = np.sqrt((4.0 * l * l - 1.0) / (l * l - m * m))
            backward = np.sqrt(((l - 1.0) ** 2 - m * m) / (4.0 * (l - 1.0) ** 2 - 1.0))
            legendre[l, m] = factor * (
                cos_polar * legendre[l - 1, m] - backward * legendre[l - 2, m]
            )
    columns = []
    for l in range(order + 1):
        for m in range(-l, l + 1):
            if m > 0:
                columns.append(np.sqrt(2.0) * legendre[l, m] * np.cos(m * az_grid))
            elif m < 0:
                columns.append(np.sqrt(2.0) * legendre[l, -m] * np.sin(-m * az_grid))
            else:
                columns.append(legendre[l, 0])
    return np.stack(columns, axis=1)


def each(count, body):
    if count <= 16:
        for i in range(count):
            body(i)
    else:
        def step(i, carry):
            body(i)
            return carry

        lax.fori_loop(0, count, step, 0)


def rounded(value):
    return value.astype(BF16).astype(F32)


def split3(value):
    first = rounded(value)
    rest = value - first
    second = rounded(rest)
    return first, second, rounded(rest - second)


def wall_kernel(
    cells,
    walls,
    dest_s,
    slot_s,
    pick_s,
    src_s,
    rank_s,
    owner_s,
    cell_ref,
    dest_ref,
    slot_ref,
    harm_ref,
    shape_ref,
    force_ref,
    centers_ref,
    blocks_ref,
    srcb_ref,
    couple_ref,
    tgtb_ref,
    out_ref,
    b_sc,
    a_sc,
    at_sc,
    x_sc,
    v_sc,
    s_sc,
    part_sc,
    recv_sc,
    stage_sc,
    mask_sc,
    wall_send,
    wall_recv,
    cell_send,
    cell_recv,
    ring_send,
    ring_recv,
    *step_sc,
):
    clusters = centers_ref.shape[0]
    panels = centers_ref.shape[1] // 3
    near = dest_ref.shape[1]
    group = walls * clusters
    chunks = b_sc.shape[2] // (2 * LANES)
    me_cell = lax.axis_index("cells")
    me = lax.axis_index("wall")

    def wall_peer(d):
        return lax.rem(me + d, walls)

    def cell_peer(d):
        return lax.rem(me_cell + d, cells)

    barrier = pltpu.get_barrier_semaphore()

    def greet_wall(i):
        pl.semaphore_signal(barrier, inc=1, device_id={"wall": wall_peer(i + 1)}, device_id_type=MESH)

    def greet_cell(i):
        pl.semaphore_signal(barrier, inc=1, device_id={"cells": cell_peer(i + 1)}, device_id_type=MESH)

    each(walls - 1, greet_wall)
    each(cells - 1, greet_cell)

    for s in range(clusters):
        x_sc[me * clusters + s] = centers_ref[s : s + 1, :]

    def column(row):
        size = row.shape[1]
        down = lax.broadcasted_iota(jnp.int32, (size, size), 0)
        across = lax.broadcasted_iota(jnp.int32, (size, size), 1)
        return jnp.sum(jnp.where(down == across, row, 0.0), axis=1, keepdims=True)

    cell_col = column(cell_ref[...].astype(F32))
    cell_count = shape_ref.shape[2]
    lane_cell = lax.broadcasted_iota(jnp.int32, (near, cell_count), 1).astype(F32)
    onehot = (lane_cell == cell_col).astype(BF16)

    def on_grid(ref, a):
        picked = lax.dot_general(onehot, ref[a], NT, preferred_element_type=F32).astype(BF16)
        return rounded(jnp.dot(picked, harm_ref[...], preferred_element_type=F32))

    def put(row, half, value):
        for j in range(chunks):
            at = (2 * j + half) * LANES
            b_sc[:, row, at : at + LANES] = value[:, j * LANES : (j + 1) * LANES]

    points = [on_grid(shape_ref, a) for a in range(3)]

    pl.semaphore_wait(barrier, walls + cells - 2)

    def wall_copy(phase, d, src, dst):
        return pltpu.make_async_remote_copy(
            src_ref=src,
            dst_ref=dst,
            send_sem=wall_send.at[phase, d],
            recv_sem=wall_recv.at[phase, d],
            device_id={"wall": wall_peer(d)},
            device_id_type=MESH,
        )

    own = pl.ds(me * clusters, clusters)

    def center_copy(d):
        return wall_copy(0, d, x_sc.at[own], x_sc.at[own])

    each(walls - 1, lambda i: center_copy(i + 1).start())

    forces = [on_grid(force_ref, a) for a in range(3)]
    zero = jnp.zeros_like(points[0])
    one = zero + 1.0
    square = points[0] * points[0] + points[1] * points[1] + points[2] * points[2] + soft_core
    inner = points[0] * forces[0] + points[1] * forces[1] + points[2] * forces[2]
    for a in range(3):
        double = points[a] * -2.0
        for half, value in ((0, double), (1, forces[a])):
            put(a, half, value)
            put(3 + a, half, value)
        put(12 + a, 0, points[a])
        put(12 + a, 1, zero)
        put(9 + a, 0, one)
        put(9 + a, 1, zero)
    for a, (sq, inn) in enumerate(zip(split3(square), split3(inner))):
        put(6 + a, 0, sq)
        put(6 + a, 1, -inn)
    put(15, 0, zero)
    put(15, 1, zero)

    rank_size = couple_ref.shape[2]
    far_blocks = couple_ref.shape[1]
    level_i = lax.broadcasted_iota(jnp.int32, (rank_size, rank_size), 0)
    level_j = lax.broadcasted_iota(jnp.int32, (rank_size, rank_size), 1)
    level = jnp.maximum(level_i, level_j)
    for t in range(clusters):
        for b in range(far_blocks):
            mask_sc[t, b] = jnp.where(level < rank_s[t, b], couple_ref[t, b], 0.0)

    each(walls - 1, lambda i: center_copy(i + 1).wait())

    def make_panels(t):
        for a in range(3):
            spot = x_sc[t][:, a * panels : (a + 1) * panels]
            first = rounded(spot)
            second = rounded(spot - first)
            held = first + second
            at_sc[a : a + 1, :] = first
            at_sc[3 + a : 4 + a, :] = second
            norm = held * held if a == 0 else norm + held * held
        for a, value in enumerate(split3(norm)):
            at_sc[9 + a : 10 + a, :] = value
        a_sc[t] = jnp.transpose(at_sc[...]).astype(BF16)

    at_sc[6:9, :] = jnp.ones((3, panels), F32)
    at_sc[12:16, :] = jnp.zeros((4, panels), F32)
    each(group, make_panels)

    def pair_row(r, carry):
        target = dest_s[r] * clusters + slot_s[r]
        panel = a_sc[target]
        total = jnp.zeros((ROWS, panels), F32)
        for j in range(chunks):
            rows = b_sc[r, :, 2 * j * LANES : 2 * (j + 1) * LANES].astype(BF16)
            both = jnp.dot(panel, rows, preferred_element_type=F32)
            inverse = lax.rsqrt(both[:, :LANES])
            along = both[:, LANES:] * (inverse * inverse * inverse)
            pair = jnp.concatenate([along.astype(BF16), inverse.astype(BF16)], axis=1)
            total += lax.dot_general(rows, pair, NT, preferred_element_type=F32)
        v_sc[pl.ds(pl.multiple_of(r * ROWS, ROWS), ROWS), :] = total
        return carry

    lax.fori_loop(0, near, pair_row, 0, unroll=2)

    flat = near * ROWS
    target_row = (dest_ref[...] * clusters + slot_ref[...]).astype(F32)
    spread = (
        lax.shift_right_logical(lax.broadcasted_iota(jnp.int32, (near, flat), 1), 4)
        == lax.broadcasted_iota(jnp.int32, (near, flat), 0)
    ).astype(F32)
    target_flat = jnp.dot(
        jnp.broadcast_to(target_row, (8, near)), spread, precision=HIGHEST, preferred_element_type=F32
    )[0:1]
    down = lax.broadcasted_iota(jnp.int32, (group * 8, flat), 0)
    across = lax.broadcasted_iota(jnp.int32, (group * 8, flat), 1)
    kind = down & 7
    source = across & (ROWS - 1)
    same = lax.shift_right_logical(down, 3).astype(F32) == target_flat
    use = ((kind < 3) & ((source == kind) | (source == kind + 12))) | ((kind == 3) & (source == 9))
    select = (same & use).astype(F32)
    s_sc[...] = jnp.dot(select, v_sc[...], precision=HIGHEST, preferred_element_type=F32).reshape(
        group, 8, panels
    )

    def make_part(t):
        for a in range(3):
            lanes = slice(a * panels, (a + 1) * panels)
            part_sc[t, :, lanes] = -stokes_scale * (
                s_sc[t, a : a + 1, :] + x_sc[t, :, lanes] * s_sc[t, 3:4, :]
            )

    each(group, make_part)

    def part_copy(d):
        return wall_copy(
            1, d, part_sc.at[pl.ds(wall_peer(d) * clusters, clusters)], recv_sc.at[me]
        )

    each(walls - 1, lambda i: part_copy(i + 1).start())
    recv_sc[me] = part_sc[own]
    each(walls - 1, lambda i: part_copy(i + 1).wait())
    total = jnp.sum(recv_sc[...], axis=0)
    rhs = [total[t] for t in range(clusters)]

    flat_i = lax.broadcasted_iota(jnp.int32, (rank_size, LANES), 0)
    flat_j = lax.broadcasted_iota(jnp.int32, (rank_size, LANES), 1)
    diagonal = flat_i == flat_j
    first_row = me_cell * group

    def apply_block(t, b, vector):
        low = jnp.broadcast_to(vector.astype(BF16), (ROWS, vector.shape[1]))
        return lax.dot_general(low, blocks_ref[t, b], NT, preferred_element_type=F32)[0:1]

    density = rhs
    for step in range(ITERS):
        table_sc, nbr_sc = step_sc[2 * step : 2 * step + 2]
        ring = pltpu.make_async_remote_copy(
            src_ref=stage_sc.at[step],
            dst_ref=nbr_sc,
            send_sem=ring_send.at[step],
            recv_sem=ring_recv.at[step],
            device_id={"wall": wall_peer(1)},
            device_id_type=MESH,
        )
        for t in range(clusters):
            coef = jnp.sum(srcb_ref[t] * density[t], axis=1, keepdims=True)
            table_sc[first_row + me * clusters + t] = jnp.sum(
                jnp.where(diagonal, coef, 0.0), axis=0, keepdims=True
            )
            stage_sc[step, t] = density[t]
        mine = table_sc.at[pl.ds(first_row + me * clusters, clusters)]

        def coef_copy(d):
            return wall_copy(2 + step, d, mine, mine)

        each(walls - 1, lambda i: coef_copy(i + 1).start())
        ring.start()
        near_term = [apply_block(t, 0, density[t]) for t in range(clusters)]
        each(walls - 1, lambda i: coef_copy(i + 1).wait())
        block = table_sc.at[pl.ds(first_row, group)]

        def block_copy(d):
            return pltpu.make_async_remote_copy(
                src_ref=block,
                dst_ref=block,
                send_sem=cell_send.at[step, d],
                recv_sem=cell_recv.at[step, d],
                device_id={"cells": cell_peer(d)},
                device_id_type=MESH,
            )

        each(cells - 1, lambda i: block_copy(i + 1).start())
        ring.wait()
        near_term = [
            near_term[t] + apply_block(t, 1, nbr_sc[pick_s[t]]) for t in range(clusters)
        ]
        each(cells - 1, lambda i: block_copy(i + 1).wait())
        fresh = []
        for t in range(clusters):
            mixed = jnp.zeros((rank_size, rank_size), F32)
            for b in range(far_blocks):
                row = table_sc[owner_s[src_s[t, b]]]
                mixed += mask_sc[t, b] * row[:, :rank_size]
            mixed = jnp.sum(mixed, axis=1, keepdims=True)
            far_term = jnp.sum(tgtb_ref[t] * mixed, axis=0, keepdims=True)
            fresh.append(rhs[t] - near_term[t] - far_term)
        density = fresh
    for t in range(clusters):
        out_ref[t : t + 1, :] = density[t]


def local(
    shape_coef,
    force_coef,
    near_cell,
    near_dest,
    near_slot,
    panel_centers,
    near_blocks,
    near_pick,
    src_basis,
    far_couple,
    far_src,
    far_rank,
    tgt_basis,
    cluster_slot,
):
    cells = lax.axis_size("cells")
    walls = lax.axis_size("wall")
    near = near_cell.shape[0]
    clusters, width = panel_centers.shape
    panels = width // 3
    group = walls * clusters
    harmonic_host = harmonics(ORDER)
    harmonic = jnp.asarray(harmonic_host, F32).astype(BF16)
    grid_points = harmonic_host.shape[0]
    padded = -(-grid_points // LANES) * LANES
    harmonic_t = jnp.asarray(
        np.pad(harmonic_host.T, ((0, 0), (0, padded - grid_points))), F32
    ).astype(BF16)
    surface = jnp.einsum(
        "qs,asc->aqc", harmonic, shape_coef, preferred_element_type=F32
    ).astype(BF16)
    smem = pl.BlockSpec(memory_space=pltpu.SMEM)
    vmem = pl.BlockSpec(memory_space=pltpu.VMEM)
    density = pl.pallas_call(
        functools.partial(wall_kernel, cells, walls),
        out_shape=jax.ShapeDtypeStruct((clusters, width), F32),
        in_specs=[smem] * 6 + [vmem] * 11,
        out_specs=vmem,
        scratch_shapes=[
            pltpu.VMEM((near, ROWS, 2 * padded), F32),
            pltpu.VMEM((group, panels, ROWS), BF16),
            pltpu.VMEM((ROWS, panels), F32),
            pltpu.VMEM((group, 1, width), F32),
            pltpu.VMEM((near * ROWS, panels), F32),
            pltpu.VMEM((group, 8, panels), F32),
            pltpu.VMEM((group, 1, width), F32),
            pltpu.VMEM((walls, clusters, 1, width), F32),
            pltpu.VMEM((ITERS, clusters, 1, width), F32),
            pltpu.VMEM(far_couple.shape, F32),
            pltpu.SemaphoreType.DMA((2 + ITERS, walls)),
            pltpu.SemaphoreType.DMA((2 + ITERS, walls)),
            pltpu.SemaphoreType.DMA((ITERS, cells)),
            pltpu.SemaphoreType.DMA((ITERS, cells)),
            pltpu.SemaphoreType.DMA((ITERS,)),
            pltpu.SemaphoreType.DMA((ITERS,)),
        ]
        + [
            pltpu.VMEM((cells * group, 1, LANES), F32),
            pltpu.VMEM((clusters, 1, width), F32),
        ]
        * ITERS,
        compiler_params=pltpu.CompilerParams(
            collective_id=0, has_side_effects=True, vmem_limit_bytes=48 * 1024 * 1024
        ),
    )(
        near_dest,
        near_slot,
        near_pick,
        far_src,
        far_rank,
        cluster_slot,
        near_cell[None, :],
        near_dest[None, :],
        near_slot[None, :],
        harmonic_t,
        shape_coef,
        force_coef,
        panel_centers,
        near_blocks,
        jnp.transpose(src_basis, (0, 2, 1)),
        far_couple,
        tgt_basis,
    )
    return (surface, density)


def solution(mesh):
    return jax.shard_map(
        local,
        mesh=mesh,
        in_specs=(
            P(None, None, ("cells", "wall")),
            P(None, None, ("cells", "wall")),
            P(("cells", "wall")),
            P(("cells", "wall")),
            P(("cells", "wall")),
            P(("cells", "wall"), None),
            P(("cells", "wall"), None, None, None),
            P(("cells", "wall")),
            P(("cells", "wall"), None, None),
            P(("cells", "wall"), None, None, None),
            P(("cells", "wall"), None),
            P(("cells", "wall"), None),
            P(("cells", "wall"), None, None),
            P(),
        ),
        out_specs=(P(None, None, ("cells", "wall")), P(("cells", "wall"), None)),
        check_vma=False,
    )
```

time: 179 us -> 69 us (0.39)
  blocking collectives: 90.4 us -> 0 us
  Pallas kernels: 0 us -> 53.5 us
  other arithmetic: 43.9 us -> 0 us
  starting transfers between devices: 11.2 us -> 0 us
  waiting for transfers between devices: 8.18 us -> 0 us
  local copies, waits for them, and re-layouts: 19 us -> 12.7 us
  matrix products: 4.49 us -> 1.57 us
    all_gather x3 -> x0, blocking collectives: 90.4 us -> none  [the longest x2 75.9 us: local(): lax.all_gather(coefficients, ('cells', 'wall'), axis=0, tiled=True)]
    pallas_call x0 -> x1, Pallas kernels: none -> 53.5 us  [local(): pl.pallas_call(functools.partial(wall_kernel, cells, walls), out_shape=ja...]
    reduce_sum x9 -> x0, other arithmetic: 37.6 us -> none  [the longest x8 36.8 us: kernel_block(): jnp.sum(strength[:, a, None, :] * inverse + offset[a] * along * inverse_c...]
    all_to_all x2 -> x0, starting transfers between devices: 10.8 us -> none  [the longest x1 6.33 us: local(): lax.all_to_all(id_buffer, 'wall', split_axis=0, concat_axis=0, tiled=True)]
    unnamed x24 -> x33, local copies, waits for them, and re-layouts: 2.2 us -> 12.7 us
    all_to_all x2 -> x0, waiting for transfers between devices: 8.17 us -> none  [the longest x1 8.16 us: local(): lax.all_to_all(vel_buffer, 'wall', split_axis=0, concat_axis=0, tiled=True)]
    gather x9 -> x0, local copies, waits for them, and re-layouts: 6.44 us -> none  [the longest x1 1.91 us: local(): picked = jnp.take(force_coef, near_cell, axis=2)]
    dynamic_slice x32 -> x0, local copies, waits for them, and re-layouts: 4.48 us -> none  [stokes_rows(): lax.map(kernel_block, (points.reshape(groups, width, 3, points.shape[2]),...]
  transfers between devices with their start and end apart: 4 -> 0, of which waited for: 1 -> 0; matrix products, arithmetic and copies ran while one was open for 34% -> 0% of each run, Pallas kernels for 0% -> 0%
where the time goes in v1:
time: 69 us; the launch traced here: 68.5 us
  Pallas kernels  53.5 us (78%)
  local copies, waits for them, and re-layouts  12.7 us (18%)
  matrix products  1.57 us (2%)
    pallas_call x1, Pallas kernels, local(): pl.pallas_call(functools.partial(wall_kernel, cells, walls), out_shape=ja...  53.5 us
    unnamed x33, local copies, waits for them, and re-layouts  12.7 us
    dot_general x1, matrix products, local(): jnp.einsum('qs,asc->aqc', harmonic, shape_coef, preferred_element_type=F32)  1.57 us

profile of v1, /device:TPU:0, one launch (start us, length us, event | category | flops | bytes accessed | tf_op | source)
XLA Modules:
  0.0 68.5 jit_solution(16939597650394033974)
XLA Ops:
  0.6 0.0 copy-start
  0.6 1.3 %copy-done = bf16[2,2,384,384]{3,2,1,0:T(8,128)(2,1)S(1)} copy-done((bf16[2,2,384,384]{3,2,1,0:T(8,128)(2,1)S(1)}, bf16[2,2,384,384]{3,2,1,0:T(8,128)(2,1)}, u32[]{:S(2)}) %copy-start) | copy-done | bytes 1179672
  1.9 0.0 copy-start.1
  1.9 1.0 %copy-done.1 = bf16[3,289,256]{2,1,0:T(8,128)(2,1)S(1)} copy-done((bf16[3,289,256]{2,1,0:T(8,128)(2,1)S(1)}, bf16[3,289,256]{2,1,0:T(8,128)(2,1)}, u32[]{:S(2)}) %copy-start.1) | copy-done | bytes 443928
  2.9 0.0 copy-start.2
  2.9 1.0 %copy-done.2 = bf16[3,289,256]{2,1,0:T(8,128)(2,1)S(1)} copy-done((bf16[3,289,256]{2,1,0:T(8,128)(2,1)S(1)}, bf16[3,289,256]{2,1,0:T(8,128)(2,1)}, u32[]{:S(2)}) %copy-start.2) | copy-done | bytes 443928
  3.9 0.0 copy-start.3
  3.9 1.0 %copy-done.3 = bf16[289,640]{1,0:T(8,128)(2,1)S(1)} copy-done((bf16[289,640]{1,0:T(8,128)(2,1)S(1)}, bf16[289,640]{1,0:T(8,128)(2,1)}, u32[]{:S(2)}) %copy-start.3) | copy-done | bytes 369944
  4.9 0.0 copy-start.4
  4.9 0.9 %copy-done.4 = f32[2,8,16,16]{3,2,1,0:T(8,128)S(1)} copy-done((f32[2,8,16,16]{3,2,1,0:T(8,128)S(1)}, f32[2,8,16,16]{3,2,1,0:T(8,128)}, u32[]{:S(2)}) %copy-start.4) | copy-done | bytes 16408
  5.8 0.0 copy-start.5
  5.8 0.8 %copy-done.5 = f32[2,384,16]{1,2,0:T(8,128)S(1)} copy-done((f32[2,384,16]{1,2,0:T(8,128)S(1)}, f32[2,384,16]{1,2,0:T(8,128)}, u32[]{:S(2)}) %copy-start.5) | copy-done | bytes 49176
  6.6 0.0 copy-start.6
  6.6 0.8 %copy-done.6 = f32[2,16,384]{2,1,0:T(8,128)S(1)} copy-done((f32[2,16,384]{2,1,0:T(8,128)S(1)}, f32[2,16,384]{2,1,0:T(8,128)}, u32[]{:S(2)}) %copy-start.6) | copy-done | bytes 49176
  7.4 0.0 copy-start.7
  7.4 0.7 copy-done.7
  8.1 0.0 copy-start.8
  8.1 0.7 copy-done.8
  8.8 0.0 copy-start.9
  8.8 0.7 copy-done.9
  9.4 0.0 copy-start.10
  9.4 0.7 copy-done.10
  10.1 0.7 copy-done.11
  10.8 0.0 copy-start.12
  10.8 0.7 copy-done.12
  11.4 0.0 copy-start.13
  11.4 0.7 copy-done.13
  12.1 0.7 copy-done.14
  12.8 53.5 %shard_map.167 = f32[2,384]{1,0:T(2,128)S(1)} custom-call(s32[64]{0:T(128)S(1)} %copy-done.8, s32[64]{0:T(128)S(1)} %copy-done.9, s32[2]{0:T(128)S(1)} %copy-done.12, s32[2,8]{1,0:T(2,128)S(1)} %copy-done.10, s32[2,8]{1,0:T(2,128)S(1)} %copy-done.11, s32[64]{0:T(128)S(1)} %copy-done.13, s32[1,64]{1,0:T(1,128)S(1)} %bitcast.12, s32[1,64]{1,0:T(1,128)S(1)} %bitcast.10, ...), custom_call_target="tpu_custom_call" | custom-call | tf_op jit(solution)/shard_map/pallas_call | solution.py:395
  66.3 0.0 copy-done.15
  66.3 1.6 %fusion = bf16[3,578,256]{2,1,0:T(8,128)(2,1)} fusion(bf16[578,289,1]{0,1,2:T(8,128)(2,1)S(1)} %copy-done.15, bf16[3,289,256]{2,1,0:T(8,128)(2,1)S(1)} %copy-done.2), kind=kOutput, calls=%fused_computation.1 | convolution fusion | flops 257020416 | bytes 1665796 | tf_op jit(solution)/shard_map/qs,asc->aqc/dot_general | solution.py:390
  67.9 0.6 copy.19
  (3 shorter events, 0.0 us)
Async XLA Ops:
  0.6 1.3 %copy-start = (bf16[2,2,384,384]{3,2,1,0:T(8,128)(2,1)S(1)}, bf16[2,2,384,384]{3,2,1,0:T(8,128)(2,1)}, u32[]{:S(2)}) copy-start(bf16[2,2,384,384]{3,2,1,0:T(8,128)(2,1)} %blocks_ref.1) | copy-start | bytes 3538948
  1.9 1.0 %copy-start.1 = (bf16[3,289,256]{2,1,0:T(8,128)(2,1)S(1)}, bf16[3,289,256]{2,1,0:T(8,128)(2,1)}, u32[]{:S(2)}) copy-start(bf16[3,289,256]{2,1,0:T(8,128)(2,1)} %force_ref.1) | copy-start | bytes 1331716
  2.9 1.0 %copy-start.2 = (bf16[3,289,256]{2,1,0:T(8,128)(2,1)S(1)}, bf16[3,289,256]{2,1,0:T(8,128)(2,1)}, u32[]{:S(2)}) copy-start(bf16[3,289,256]{2,1,0:T(8,128)(2,1)} %shape_ref.1) | copy-start | bytes 1331716
  3.9 1.0 %copy-start.3 = (bf16[289,640]{1,0:T(8,128)(2,1)S(1)}, bf16[289,640]{1,0:T(8,128)(2,1)}, u32[]{:S(2)}) copy-start(bf16[289,640]{1,0:T(8,128)(2,1)} %constant.15.harm_ref) | copy-start | bytes 1109764
  4.9 0.9 %copy-start.4 = (f32[2,8,16,16]{3,2,1,0:T(8,128)S(1)}, f32[2,8,16,16]{3,2,1,0:T(8,128)}, u32[]{:S(2)}) copy-start(f32[2,8,16,16]{3,2,1,0:T(8,128)} %couple_ref.1) | copy-start | bytes 49156
  5.8 0.8 %copy-start.5 = (f32[2,384,16]{1,2,0:T(8,128)S(1)}, f32[2,384,16]{1,2,0:T(8,128)}, u32[]{:S(2)}) copy-start(f32[2,384,16]{1,2,0:T(8,128)} %param.24) | copy-start | bytes 147460
  6.6 0.8 %copy-start.6 = (f32[2,16,384]{2,1,0:T(8,128)S(1)}, f32[2,16,384]{2,1,0:T(8,128)}, u32[]{:S(2)}) copy-start(f32[2,16,384]{2,1,0:T(8,128)} %tgtb_ref.1) | copy-start | bytes 147460
  7.4 0.7 copy-start.7
  8.1 0.7 copy-start.8
  8.8 0.7 copy-start.9
  9.4 0.7 copy-start.10
  10.1 0.7 copy-start.11
  10.8 0.7 copy-start.12
  11.4 0.7 copy-start.13
  12.1 0.7 copy-start.14
  12.8 53.6 %copy-start.15 = (bf16[578,289,1]{0,1,2:T(8,128)(2,1)S(1)}, bf16[578,289,1]{0,1,2:T(8,128)(2,1)}, u32[]{:S(2)}) copy-start(bf16[578,289,1]{0,1,2:T(8,128)(2,1)} %constant.16) | copy-start | bytes 1002256

commit v2 on v1

--- a/solution.py
+++ b/solution.py
@@ -13,6 +13,8 @@
 ITERS = 2
 LANES = 128
 ROWS = 16
+SPAN = 256
+OPERANDS = 17
 
 soft_core = 0.25
 stokes_scale = 1.0 / (8.0 * math.pi)
@@ -82,47 +84,65 @@
 def wall_kernel(
     cells,
     walls,
-    dest_s,
-    slot_s,
-    pick_s,
-    src_s,
-    rank_s,
-    owner_s,
-    cell_ref,
-    dest_ref,
-    slot_ref,
-    harm_ref,
-    shape_ref,
-    force_ref,
-    centers_ref,
-    blocks_ref,
-    srcb_ref,
-    couple_ref,
-    tgtb_ref,
-    out_ref,
-    b_sc,
-    a_sc,
-    at_sc,
-    x_sc,
-    v_sc,
-    s_sc,
-    part_sc,
-    recv_sc,
-    stage_sc,
-    mask_sc,
-    wall_send,
-    wall_recv,
-    cell_send,
-    cell_recv,
-    ring_send,
-    ring_recv,
-    *step_sc,
+    points_count,
+    *refs,
 ):
+    operands, refs = refs[:OPERANDS], refs[OPERANDS:]
+    out_ref, refs = refs[0], refs[1:]
+    held, refs = refs[:OPERANDS], refs[OPERANDS:]
+    (
+        b_sc,
+        bt_sc,
+        a_sc,
+        at_sc,
+        x_sc,
+        v_sc,
+        e_sc,
+        s_sc,
+        part_sc,
+        recv_sc,
+        stage_sc,
+        mask_sc,
+        load_sem,
+        wall_send,
+        wall_recv,
+        cell_send,
+        cell_recv,
+        ring_send,
+        ring_recv,
+        *step_sc,
+    ) = refs
+    loads = [
+        pltpu.make_async_copy(operands[i], held[i], load_sem.at[i]) for i in range(OPERANDS)
+    ]
+    (
+        cell_ref,
+        shape_ref,
+        harm_ref,
+        centers_ref,
+        force_ref,
+        dest_ref,
+        slot_ref,
+        dest_s,
+        slot_s,
+        rank_s,
+        couple_ref,
+        pick_s,
+        src_s,
+        owner_s,
+        srcb_ref,
+        tgtb_ref,
+        blocks_ref,
+    ) = held
+    for load in loads:
+        load.start()
     clusters = centers_ref.shape[0]
     panels = centers_ref.shape[1] // 3
     near = dest_ref.shape[1]
     group = walls * clusters
-    chunks = b_sc.shape[2] // (2 * LANES)
+    padded = b_sc.shape[2]
+    chunks = padded // LANES
+    batch = LANES // (2 * ROWS)
     me_cell = lax.axis_index("cells")
     me = lax.axis_index("wall")
 
@@ -142,9 +162,6 @@
 
     each(walls - 1, greet_wall)
     each(cells - 1, greet_cell)
-
-    for s in range(clusters):
-        x_sc[me * clusters + s] = centers_ref[s : s + 1, :]
 
     def column(row):
         size = row.shape[1]
@@ -152,6 +169,11 @@
         across = lax.broadcasted_iota(jnp.int32, (size, size), 1)
         return jnp.sum(jnp.where(down == across, row, 0.0), axis=1, keepdims=True)
 
+    a_sc[...] = jnp.zeros(a_sc.shape, BF16)
+    for load in loads[:4]:
+        load.wait()
+    for s in range(clusters):
+        x_sc[me * clusters + s] = centers_ref[s : s + 1, :]
     cell_col = column(cell_ref[...].astype(F32))
     cell_count = shape_ref.shape[2]
     lane_cell = lax.broadcasted_iota(jnp.int32, (near, cell_count), 1).astype(F32)
@@ -162,9 +184,7 @@
         return rounded(jnp.dot(picked, harm_ref[...], preferred_element_type=F32))
 
     def put(row, half, value):
-        for j in range(chunks):
-            at = (2 * j + half) * LANES
-            b_sc[:, row, at : at + LANES] = value[:, j * LANES : (j + 1) * LANES]
+        b_sc[:, half * ROWS + row, :] = value
 
     points = [on_grid(shape_ref, a) for a in range(3)]
 
@@ -187,6 +207,8 @@
 
     each(walls - 1, lambda i: center_copy(i + 1).start())
 
+    for load in loads[4:]:
+        load.wait()
     forces = [on_grid(force_ref, a) for a in range(3)]
     zero = jnp.zeros_like(points[0])
     one = zero + 1.0
@@ -196,16 +218,26 @@
         double = points[a] * -2.0
         for half, value in ((0, double), (1, forces[a])):
             put(a, half, value)
-            put(3 + a, half, value)
-        put(12 + a, 0, points[a])
-        put(12 + a, 1, zero)
-        put(9 + a, 0, one)
-        put(9 + a, 1, zero)
-    for a, (sq, inn) in enumerate(zip(split3(square), split3(inner))):
-        put(6 + a, 0, sq)
-        put(6 + a, 1, -inn)
-    put(15, 0, zero)
-    put(15, 1, zero)
+            put(12 + a, half, value)
+        put(8 + a, 0, points[a])
+        put(8 + a, 1, zero)
+        put(3 + a, 0, one)
+        put(3 + a, 1, zero)
+    for row, sq, inn in zip((6, 7, 15), split3(square), split3(inner)):
+        put(row, 0, sq)
+        put(row, 1, -inn)
+    put(11, 0, zero)
+    put(11, 1, zero)
+
+    def turn(g, carry):
+        for j in range(chunks):
+            width = min(LANES, points_count - j * LANES)
+            tile = b_sc[pl.ds(g * batch, batch), :, j * LANES : (j + 1) * LANES]
+            turned = jnp.transpose(tile.reshape(LANES, LANES))
+            bt_sc[g, j * LANES : j * LANES + width, :] = turned[:width].astype(BF16)
+        return carry
+
+    lax.fori_loop(0, near // batch, turn, 0)
 
     rank_size = couple_ref.shape[2]
     far_blocks = couple_ref.shape[1]
@@ -216,45 +248,10 @@
         for b in range(far_blocks):
             mask_sc[t, b] = jnp.where(level < rank_s[t, b], couple_ref[t, b], 0.0)
 
-    each(walls - 1, lambda i: center_copy(i + 1).wait())
-
-    def make_panels(t):
-        for a in range(3):
-            spot = x_sc[t][:, a * panels : (a + 1) * panels]
-            first = rounded(spot)
-            second = rounded(spot - first)
-            held = first + second
-            at_sc[a : a + 1, :] = first
-            at_sc[3 + a : 4 + a, :] = second
-            norm = held * held if a == 0 else norm + held * held
-        for a, value in enumerate(split3(norm)):
-            at_sc[9 + a : 10 + a, :] = value
-        a_sc[t] = jnp.transpose(at_sc[...]).astype(BF16)
-
-    at_sc[6:9, :] = jnp.ones((3, panels), F32)
-    at_sc[12:16, :] = jnp.zeros((4, panels), F32)
-    each(group, make_panels)
-
-    def pair_row(r, carry):
-        target = dest_s[r] * clusters + slot_s[r]
-        panel = a_sc[target]
-        total = jnp.zeros((ROWS, panels), F32)
-        for j in range(chunks):
-            rows = b_sc[r, :, 2 * j * LANES : 2 * (j + 1) * LANES].astype(BF16)
-            both = jnp.dot(panel, rows, preferred_element_type=F32)
-            inverse = lax.rsqrt(both[:, :LANES])
-            along = both[:, LANES:] * (inverse * inverse * inverse)
-            pair = jnp.concatenate([along.astype(BF16), inverse.astype(BF16)], axis=1)
-            total += lax.dot_general(rows, pair, NT, preferred_element_type=F32)
-        v_sc[pl.ds(pl.multiple_of(r * ROWS, ROWS), ROWS), :] = total
-        return carry
-
-    lax.fori_loop(0, near, pair_row, 0, unroll=2)
-
-    flat = near * ROWS
+    flat = near * 8
     target_row = (dest_ref[...] * clusters + slot_ref[...]).astype(F32)
     spread = (
-        lax.shift_right_logical(lax.broadcasted_iota(jnp.int32, (near, flat), 1), 4)
+        lax.shift_right_logical(lax.broadcasted_iota(jnp.int32, (near, flat), 1), 3)
         == lax.broadcasted_iota(jnp.int32, (near, flat), 0)
     ).astype(F32)
     target_flat = jnp.dot(
@@ -262,14 +259,61 @@
     )[0:1]
     down = lax.broadcasted_iota(jnp.int32, (group * 8, flat), 0)
     across = lax.broadcasted_iota(jnp.int32, (group * 8, flat), 1)
-    kind = down & 7
-    source = across & (ROWS - 1)
     same = lax.shift_right_logical(down, 3).astype(F32) == target_flat
-    use = ((kind < 3) & ((source == kind) | (source == kind + 12))) | ((kind == 3) & (source == 9))
-    select = (same & use).astype(F32)
-    s_sc[...] = jnp.dot(select, v_sc[...], precision=HIGHEST, preferred_element_type=F32).reshape(
-        group, 8, panels
-    )
+    e_sc[...] = jnp.where(same & ((down & 7) == (across & 7)), 1.0, 0.0).astype(BF16)
+
+    at_sc[6:12, :] = jnp.ones((6, panels), F32)
+    at_sc[8:12, :] = jnp.zeros((4, panels), F32)
+    at_sc[15:16, :] = jnp.ones((1, panels), F32)
+    each(walls - 1, lambda i: center_copy(i + 1).wait())
+
+    def make_panels(t):
+        for a in range(3):
+            spot = x_sc[t][:, a * panels : (a + 1) * panels]
+            first = rounded(spot)
+            second = rounded(spot - first)
+            whole = first + second
+            at_sc[a : a + 1, :] = first
+            at_sc[12 + a : 13 + a, :] = second
+            norm = whole * whole if a == 0 else norm + whole * whole
+        for a, value in enumerate(split3(norm)):
+            at_sc[3 + a : 4 + a, :] = value
+        rows = at_sc[...].astype(BF16)
+        a_sc[t, 0:ROWS, 0:panels] = rows
+        a_sc[t, ROWS : 2 * ROWS, panels : 2 * panels] = rows
+
+    each(group, make_panels)
+
+    empty = jnp.zeros((2 * ROWS, 2 * panels), BF16)
+
+    def pair_rows(g, carry):
+        for i in range(batch):
+            r = g * batch + i
+            panel = a_sc[dest_s[r] * clusters + slot_s[r]]
+            weights = jnp.concatenate([panel if k == i else empty for k in range(batch)], axis=0)
+            rows = b_sc[r].astype(BF16)
+            total = jnp.zeros((2 * ROWS, 2 * panels), F32)
+            for start in range(0, points_count, SPAN):
+                stop = min(start + SPAN, points_count)
+                both = jnp.dot(bt_sc[g, start:stop, :], weights, preferred_element_type=F32)
+                inverse = lax.rsqrt(both[:, :panels])
+                along = both[:, panels:] * (inverse * inverse * inverse)
+                pair = jnp.concatenate([along.astype(BF16), inverse.astype(BF16)], axis=1)
+                total += jnp.dot(rows[:, start:stop], pair, preferred_element_type=F32)
+            summed = total[:ROWS, :panels] + total[ROWS:, panels:]
+            v_sc[pl.ds(pl.multiple_of(r * 8, 8), 8), :] = summed[:8] + summed[8:]
+        return carry
+
+    lax.fori_loop(0, near // batch, pair_rows, 0)
+
+    value = v_sc[...]
+    high = value.astype(BF16)
+    low_part = (value - high.astype(F32)).astype(BF16)
+    select = e_sc[...]
+    s_sc[...] = (
+        jnp.dot(select, high, preferred_element_type=F32)
+        + jnp.dot(select, low_part, preferred_element_type=F32)
+    ).reshape(group, 8, panels)
 
     def make_part(t):
         for a in range(3):
@@ -390,24 +434,50 @@
     surface = jnp.einsum(
         "qs,asc->aqc", harmonic, shape_coef, preferred_element_type=F32
     ).astype(BF16)
-    smem = pl.BlockSpec(memory_space=pltpu.SMEM)
-    vmem = pl.BlockSpec(memory_space=pltpu.VMEM)
+    points_count = -(-grid_points // 16) * 16
+    operands = (
+        near_cell[None, :],
+        shape_coef,
+        harmonic_t,
+        panel_centers,
+        force_coef,
+        near_dest[None, :],
+        near_slot[None, :],
+        near_dest,
+        near_slot,
+        far_rank,
+        far_couple,
+        near_pick,
+        far_src,
+        cluster_slot,
+        jnp.transpose(src_basis, (0, 2, 1)),
+        tgt_basis,
+        near_blocks,
+    )
+    scalars = (7, 8, 9, 11, 12, 13)
     density = pl.pallas_call(
-        functools.partial(wall_kernel, cells, walls),
+        functools.partial(wall_kernel, cells, walls, points_count),
         out_shape=jax.ShapeDtypeStruct((clusters, width), F32),
-        in_specs=[smem] * 6 + [vmem] * 11,
-        out_specs=vmem,
+        in_specs=[pl.BlockSpec(memory_space=pltpu.HBM)] * OPERANDS,
+        out_specs=pl.BlockSpec(memory_space=pltpu.VMEM),
         scratch_shapes=[
-            pltpu.VMEM((near, ROWS, 2 * padded), F32),
-            pltpu.VMEM((group, panels, ROWS), BF16),
+            (pltpu.SMEM if i in scalars else pltpu.VMEM)(array.shape, array.dtype)
+            for i, array in enumerate(operands)
+        ]
+        + [
+            pltpu.VMEM((near, 2 * ROWS, padded), F32),
+            pltpu.VMEM((near * 2 * ROWS // LANES, points_count, LANES), BF16),
+            pltpu.VMEM((group, 2 * ROWS, 2 * panels), BF16),
             pltpu.VMEM((ROWS, panels), F32),
             pltpu.VMEM((group, 1, width), F32),
-            pltpu.VMEM((near * ROWS, panels), F32),
+            pltpu.VMEM((near * 8, panels), F32),
+            pltpu.VMEM((group * 8, near * 8), BF16),
             pltpu.VMEM((group, 8, panels), F32),
             pltpu.VMEM((group, 1, width), F32),
             pltpu.VMEM((walls, clusters, 1, width), F32),
             pltpu.VMEM((ITERS, clusters, 1, width), F32),
             pltpu.VMEM(far_couple.shape, F32),
+            pltpu.SemaphoreType.DMA((OPERANDS,)),
             pltpu.SemaphoreType.DMA((2 + ITERS, walls)),
             pltpu.SemaphoreType.DMA((2 + ITERS, walls)),
             pltpu.SemaphoreType.DMA((ITERS, cells)),
@@ -421,27 +491,9 @@
         ]
         * ITERS,
         compiler_params=pltpu.CompilerParams(
-            collective_id=0, has_side_effects=True, vmem_limit_bytes=48 * 1024 * 1024
+            collective_id=0, has_side_effects=True, vmem_limit_bytes=60 * 1024 * 1024
         ),
-    )(
-        near_dest,
-        near_slot,
-        near_pick,
-        far_src,
-        far_rank,
-        cluster_slot,
-        near_cell[None, :],
-        near_dest[None, :],
-        near_slot[None, :],
-        harmonic_t,
-        shape_coef,
-        force_coef,
-        panel_centers,
-        near_blocks,
-        jnp.transpose(src_basis, (0, 2, 1)),
-        far_couple,
-        tgt_basis,
-    )
+    )(*operands)
     return (surface, density)
 
 

time: 69 us -> 51.3 us (0.74)
  local copies, waits for them, and re-layouts: 12.7 us -> 0.59 us
  Pallas kernels: 53.5 us -> 48.3 us
    unnamed x33 -> x7, local copies, waits for them, and re-layouts: 12.7 us -> 0.59 us
    pallas_call x1, Pallas kernels: 53.5 us -> 48.3 us  [local(): pl.pallas_call(functools.partial(wall_kernel, cells, walls, points_count)...]
where the time goes in v2:
time: 51.3 us; the launch traced here: 51.1 us
  Pallas kernels  48.3 us (94%)
  matrix products  1.58 us (3%)
  between operations  0.68 us (1%)
  local copies, waits for them, and re-layouts  0.59 us (1%)
    pallas_call x1, Pallas kernels, local(): pl.pallas_call(functools.partial(wall_kernel, cells, walls, points_count)...  48.3 us
    dot_general x1, matrix products, local(): jnp.einsum('qs,asc->aqc', harmonic, shape_coef, preferred_element_type=F32)  1.58 us

profile of v2, /device:TPU:0, one launch (start us, length us, event | category | flops | bytes accessed | tf_op | source)
XLA Modules:
  0.0 51.1 jit_solution(17863199017783762280)
XLA Ops:
  0.6 0.0 copy-start
  0.6 0.0 copy-start.2
  0.7 48.3 %shard_map.167 = f32[2,384]{1,0:T(2,128)} custom-call(s32[1,64]{1,0:T(1,128)} %bitcast.12, bf16[3,289,256]{2,1,0:T(8,128)(2,1)} %refs_1_.1, bf16[289,640]{1,0:T(8,128)(2,1)} %constant.15.refs_2_, f32[2,384]{1,0:T(2,128)} %refs_3_.1, bf16[3,289,256]{2,1,0:T(8,128)(2,1)} %refs_4_.1, s32[1,64]{1,0:T(1,128)} %bitcast.10, s32[1,64]{1,0:T(1,128)} %bitcast.11, ...), custom_call_target="tpu_custom_call" | custom-call | tf_op jit(solution)/shard_map/pallas_call | solution.py:458
  48.9 0.0 copy-done
  49.0 0.0 copy-done.2
  49.0 0.0 copy-start.1
  49.0 1.6 %fusion = bf16[3,578,256]{2,1,0:T(8,128)(2,1)} fusion(bf16[578,289,1]{0,1,2:T(8,128)(2,1)S(1)} %copy-done.2, bf16[3,289,256]{2,1,0:T(8,128)(2,1)S(1)} %copy-done), kind=kOutput, calls=%fused_computation.1 | convolution fusion | flops 257020416 | bytes 1665796 | tf_op jit(solution)/shard_map/qs,asc->aqc/dot_general | solution.py:434
  50.6 0.0 copy-done.1
  50.6 0.6 %copy.19 = f32[2,384]{1,0:T(2,128)} copy(f32[2,384]{1,0:T(2,128)S(1)} %copy-done.1) | data formatting | bytes 6144
Async XLA Ops:
  0.6 48.3 %copy-start = (bf16[3,289,256]{2,1,0:T(8,128)(2,1)S(1)}, bf16[3,289,256]{2,1,0:T(8,128)(2,1)}, u32[]{:S(2)}) copy-start(bf16[3,289,256]{2,1,0:T(8,128)(2,1)} %refs_1_.1) | copy-start | bytes 1331716
  0.6 48.3 %copy-start.2 = (bf16[578,289,1]{0,1,2:T(8,128)(2,1)S(1)}, bf16[578,289,1]{0,1,2:T(8,128)(2,1)}, u32[]{:S(2)}) copy-start(bf16[578,289,1]{0,1,2:T(8,128)(2,1)} %constant.16) | copy-start | bytes 1002256
  49.0 1.6 %copy-start.1 = (f32[2,384]{1,0:T(2,128)S(1)}, f32[2,384]{1,0:T(2,128)}, u32[]{:S(2)}) copy-start(f32[2,384]{1,0:T(2,128)} %shard_map.167) | copy-start | bytes 9220

commit v3 on v2

--- a/solution.py
+++ b/solution.py
@@ -59,7 +59,7 @@
 
 
 def each(count, body):
-    if count <= 16:
+    if count <= 32:
         for i in range(count):
             body(i)
     else:
@@ -160,8 +160,21 @@
     def greet_cell(i):
         pl.semaphore_signal(barrier, inc=1, device_id={"cells": cell_peer(i + 1)}, device_id_type=MESH)
 
-    each(walls - 1, greet_wall)
-    each(cells - 1, greet_cell)
+    devices = cells * walls
+    direct = devices <= 64
+
+    def any_peer(d):
+        peer = lax.rem(me_cell * walls + me + d, devices)
+        return {"cells": lax.div(peer, walls), "wall": lax.rem(peer, walls)}
+
+    def greet_any(i):
+        pl.semaphore_signal(barrier, inc=1, device_id=any_peer(i + 1), device_id_type=MESH)
+
+    if direct:
+        each(devices - 1, greet_any)
+    else:
+        each(walls - 1, greet_wall)
+        each(cells - 1, greet_cell)
 
     def column(row):
         size = row.shape[1]
@@ -179,16 +192,18 @@
     lane_cell = lax.broadcasted_iota(jnp.int32, (near, cell_count), 1).astype(F32)
     onehot = (lane_cell == cell_col).astype(BF16)
 
-    def on_grid(ref, a):
-        picked = lax.dot_general(onehot, ref[a], NT, preferred_element_type=F32).astype(BF16)
-        return rounded(jnp.dot(picked, harm_ref[...], preferred_element_type=F32))
+    def pick(ref):
+        return [
+            lax.dot_general(onehot, ref[a], NT, preferred_element_type=F32).astype(BF16)
+            for a in range(3)
+        ]
 
     def put(row, half, value):
         b_sc[:, half * ROWS + row, :] = value
 
-    points = [on_grid(shape_ref, a) for a in range(3)]
-
-    pl.semaphore_wait(barrier, walls + cells - 2)
+    picked = pick(shape_ref)
+
+    pl.semaphore_wait(barrier, devices - 1 if direct else walls + cells - 2)
 
     def wall_copy(phase, d, src, dst):
         return pltpu.make_async_remote_copy(
@@ -209,7 +224,10 @@
 
     for load in loads[4:]:
         load.wait()
-    forces = [on_grid(force_ref, a) for a in range(3)]
+    picked = jnp.concatenate(picked + pick(force_ref), axis=0)
+    grid = rounded(jnp.dot(picked, harm_ref[...], preferred_element_type=F32))
+    points = [grid[a * near : (a + 1) * near] for a in range(3)]
+    forces = [grid[a * near : (a + 1) * near] for a in range(3, 6)]
     zero = jnp.zeros_like(points[0])
     one = zero + 1.0
     square = points[0] * points[0] + points[1] * points[1] + points[2] * points[2] + soft_core
@@ -233,8 +251,8 @@
         for j in range(chunks):
             width = min(LANES, points_count - j * LANES)
             tile = b_sc[pl.ds(g * batch, batch), :, j * LANES : (j + 1) * LANES]
-            turned = jnp.transpose(tile.reshape(LANES, LANES))
-            bt_sc[g, j * LANES : j * LANES + width, :] = turned[:width].astype(BF16)
+            turned = jnp.transpose(tile.reshape(LANES, LANES).astype(BF16))
+            bt_sc[g, j * LANES : j * LANES + width, :] = turned[:width]
         return carry
 
     lax.fori_loop(0, near // batch, turn, 0)
@@ -262,9 +280,8 @@
     same = lax.shift_right_logical(down, 3).astype(F32) == target_flat
     e_sc[...] = jnp.where(same & ((down & 7) == (across & 7)), 1.0, 0.0).astype(BF16)
 
-    at_sc[6:12, :] = jnp.ones((6, panels), F32)
-    at_sc[8:12, :] = jnp.zeros((4, panels), F32)
-    at_sc[15:16, :] = jnp.ones((1, panels), F32)
+    kind = lax.broadcasted_iota(jnp.int32, (group, ROWS, panels), 1)
+    at_sc[...] = jnp.where((kind == 6) | (kind == 7) | (kind == 15), 1.0, 0.0)
     each(walls - 1, lambda i: center_copy(i + 1).wait())
 
     def make_panels(t):
@@ -273,12 +290,12 @@
             first = rounded(spot)
             second = rounded(spot - first)
             whole = first + second
-            at_sc[a : a + 1, :] = first
-            at_sc[12 + a : 13 + a, :] = second
+            at_sc[t, a : a + 1, :] = first
+            at_sc[t, 12 + a : 13 + a, :] = second
             norm = whole * whole if a == 0 else norm + whole * whole
         for a, value in enumerate(split3(norm)):
-            at_sc[3 + a : 4 + a, :] = value
-        rows = at_sc[...].astype(BF16)
+            at_sc[t, 3 + a : 4 + a, :] = value
+        rows = at_sc[t].astype(BF16)
         a_sc[t, 0:ROWS, 0:panels] = rows
         a_sc[t, ROWS : 2 * ROWS, panels : 2 * panels] = rows
 
@@ -293,9 +310,10 @@
             weights = jnp.concatenate([panel if k == i else empty for k in range(batch)], axis=0)
             rows = b_sc[r].astype(BF16)
             total = jnp.zeros((2 * ROWS, 2 * panels), F32)
+            whole = jnp.dot(bt_sc[g], weights, preferred_element_type=F32)
             for start in range(0, points_count, SPAN):
                 stop = min(start + SPAN, points_count)
-                both = jnp.dot(bt_sc[g, start:stop, :], weights, preferred_element_type=F32)
+                both = whole[start:stop]
                 inverse = lax.rsqrt(both[:, :panels])
                 along = both[:, panels:] * (inverse * inverse * inverse)
                 pair = jnp.concatenate([along.astype(BF16), inverse.astype(BF16)], axis=1)
@@ -366,10 +384,16 @@
         def coef_copy(d):
             return wall_copy(2 + step, d, mine, mine)
 
-        each(walls - 1, lambda i: coef_copy(i + 1).start())
-        ring.start()
-        near_term = [apply_block(t, 0, density[t]) for t in range(clusters)]
-        each(walls - 1, lambda i: coef_copy(i + 1).wait())
+        def any_copy(d, rows):
+            return pltpu.make_async_remote_copy(
+                src_ref=rows,
+                dst_ref=rows,
+                send_sem=cell_send.at[step, 0],
+                recv_sem=cell_recv.at[step, 0],
+                device_id=any_peer(d),
+                device_id_type=MESH,
+            )
+
         block = table_sc.at[pl.ds(first_row, group)]
 
         def block_copy(d):
@@ -382,12 +406,23 @@
                 device_id_type=MESH,
             )
 
-        each(cells - 1, lambda i: block_copy(i + 1).start())
+        ring.start()
+        if direct:
+            each(devices - 1, lambda i: any_copy(i + 1, mine).start())
+        else:
+            each(walls - 1, lambda i: coef_copy(i + 1).start())
+        near_term = [apply_block(t, 0, density[t]) for t in range(clusters)]
+        if not direct:
+            each(walls - 1, lambda i: coef_copy(i + 1).wait())
+            each(cells - 1, lambda i: block_copy(i + 1).start())
         ring.wait()
         near_term = [
             near_term[t] + apply_block(t, 1, nbr_sc[pick_s[t]]) for t in range(clusters)
         ]
-        each(cells - 1, lambda i: block_copy(i + 1).wait())
+        if direct:
+            any_copy(1, table_sc.at[pl.ds(0, (devices - 1) * clusters)]).wait()
+        else:
+            each(cells - 1, lambda i: block_copy(i + 1).wait())
         fresh = []
         for t in range(clusters):
             mixed = jnp.zeros((rank_size, rank_size), F32)
@@ -468,7 +503,7 @@
             pltpu.VMEM((near, 2 * ROWS, padded), F32),
             pltpu.VMEM((near * 2 * ROWS // LANES, points_count, LANES), BF16),
             pltpu.VMEM((group, 2 * ROWS, 2 * panels), BF16),
-            pltpu.VMEM((ROWS, panels), F32),
+            pltpu.VMEM((group, ROWS, panels), F32),
             pltpu.VMEM((group, 1, width), F32),
             pltpu.VMEM((near * 8, panels), F32),
             pltpu.VMEM((group * 8, near * 8), BF16),

time: 51.3 us -> 50.6 us (0.986)
  Pallas kernels: 48.3 us -> 47.6 us
    pallas_call x1, Pallas kernels: 48.3 us -> 47.6 us  [local(): pl.pallas_call(functools.partial(wall_kernel, cells, walls, points_count)...]
where the time goes in v3:
time: 50.6 us; the launch traced here: 50.4 us
  Pallas kernels  47.6 us (94%)
  matrix products  1.58 us (3%)
  between operations  0.68 us (1%)
  local copies, waits for them, and re-layouts  0.59 us (1%)
    pallas_call x1, Pallas kernels, local(): pl.pallas_call(functools.partial(wall_kernel, cells, walls, points_count)...  47.6 us
    dot_general x1, matrix products, local(): jnp.einsum('qs,asc->aqc', harmonic, shape_coef, preferred_element_type=F32)  1.58 us

profile of v3, /device:TPU:0, one launch (start us, length us, event | category | flops | bytes accessed | tf_op | source)
XLA Modules:
  0.0 50.4 jit_solution(7537997678083298019)
XLA Ops:
  0.6 0.0 copy-start
  0.6 0.0 copy-start.2
  0.7 47.6 %shard_map.167 = f32[2,384]{1,0:T(2,128)} custom-call(s32[1,64]{1,0:T(1,128)} %bitcast.12, bf16[3,289,256]{2,1,0:T(8,128)(2,1)} %refs_1_.1, bf16[289,640]{1,0:T(8,128)(2,1)} %constant.15.refs_2_, f32[2,384]{1,0:T(2,128)} %refs_3_.1, bf16[3,289,256]{2,1,0:T(8,128)(2,1)} %refs_4_.1, s32[1,64]{1,0:T(1,128)} %bitcast.10, s32[1,64]{1,0:T(1,128)} %bitcast.11, ...), custom_call_target="tpu_custom_call" | custom-call | tf_op jit(solution)/shard_map/pallas_call | solution.py:493
  48.2 0.0 copy-done
  48.2 0.0 copy-done.2
  48.3 0.0 copy-start.1
  48.3 1.6 %fusion = bf16[3,578,256]{2,1,0:T(8,128)(2,1)} fusion(bf16[578,289,1]{0,1,2:T(8,128)(2,1)S(1)} %copy-done.2, bf16[3,289,256]{2,1,0:T(8,128)(2,1)S(1)} %copy-done), kind=kOutput, calls=%fused_computation.1 | convolution fusion | flops 257020416 | bytes 1665796 | tf_op jit(solution)/shard_map/qs,asc->aqc/dot_general | solution.py:469
  49.8 0.0 copy-done.1
  49.8 0.6 %copy.19 = f32[2,384]{1,0:T(2,128)} copy(f32[2,384]{1,0:T(2,128)S(1)} %copy-done.1) | data formatting | bytes 6144
Async XLA Ops:
  0.6 47.6 %copy-start = (bf16[3,289,256]{2,1,0:T(8,128)(2,1)S(1)}, bf16[3,289,256]{2,1,0:T(8,128)(2,1)}, u32[]{:S(2)}) copy-start(bf16[3,289,256]{2,1,0:T(8,128)(2,1)} %refs_1_.1) | copy-start | bytes 1331716
  0.6 47.6 %copy-start.2 = (bf16[578,289,1]{0,1,2:T(8,128)(2,1)S(1)}, bf16[578,289,1]{0,1,2:T(8,128)(2,1)}, u32[]{:S(2)}) copy-start(bf16[578,289,1]{0,1,2:T(8,128)(2,1)} %constant.16) | copy-start | bytes 1002256
  48.3 1.6 %copy-start.1 = (f32[2,384]{1,0:T(2,128)S(1)}, f32[2,384]{1,0:T(2,128)}, u32[]{:S(2)}) copy-start(f32[2,384]{1,0:T(2,128)} %shard_map.167) | copy-start | bytes 9220

commit v4 on v3

--- a/solution.py
+++ b/solution.py
@@ -140,8 +140,7 @@
     panels = centers_ref.shape[1] // 3
     near = dest_ref.shape[1]
     group = walls * clusters
-    padded = b_sc.shape[2]
-    chunks = padded // LANES
+    chunks = b_sc.shape[0]
     batch = LANES // (2 * ROWS)
     me_cell = lax.axis_index("cells")
     me = lax.axis_index("wall")
@@ -199,7 +198,9 @@
         ]
 
     def put(row, half, value):
-        b_sc[:, half * ROWS + row, :] = value
+        for j in range(chunks):
+            rows = pl.ds(half * ROWS + row, near, stride=2 * ROWS)
+            b_sc[j, rows, :] = value[:, j * LANES : (j + 1) * LANES]
 
     picked = pick(shape_ref)
 
@@ -222,7 +223,7 @@
 
     each(walls - 1, lambda i: center_copy(i + 1).start())
 
-    for load in loads[4:]:
+    for load in loads[4:11]:
         load.wait()
     picked = jnp.concatenate(picked + pick(force_ref), axis=0)
     grid = rounded(jnp.dot(picked, harm_ref[...], preferred_element_type=F32))
@@ -250,8 +251,8 @@
     def turn(g, carry):
         for j in range(chunks):
             width = min(LANES, points_count - j * LANES)
-            tile = b_sc[pl.ds(g * batch, batch), :, j * LANES : (j + 1) * LANES]
-            turned = jnp.transpose(tile.reshape(LANES, LANES).astype(BF16))
+            tile = b_sc[j, pl.ds(pl.multiple_of(g * LANES, LANES), LANES), :]
+            turned = jnp.transpose(tile.astype(BF16))
             bt_sc[g, j * LANES : j * LANES + width, :] = turned[:width]
         return carry
 
@@ -308,7 +309,8 @@
             r = g * batch + i
             panel = a_sc[dest_s[r] * clusters + slot_s[r]]
             weights = jnp.concatenate([panel if k == i else empty for k in range(batch)], axis=0)
-            rows = b_sc[r].astype(BF16)
+            at = pl.ds(pl.multiple_of(r * 2 * ROWS, 2 * ROWS), 2 * ROWS)
+            rows = jnp.concatenate([b_sc[j, at, :] for j in range(chunks)], axis=1).astype(BF16)
             total = jnp.zeros((2 * ROWS, 2 * panels), F32)
             whole = jnp.dot(bt_sc[g], weights, preferred_element_type=F32)
             for start in range(0, points_count, SPAN):
@@ -362,6 +364,8 @@
         low = jnp.broadcast_to(vector.astype(BF16), (ROWS, vector.shape[1]))
         return lax.dot_general(low, blocks_ref[t, b], NT, preferred_element_type=F32)[0:1]
 
+    for load in loads[11:]:
+        load.wait()
     density = rhs
     for step in range(ITERS):
         table_sc, nbr_sc = step_sc[2 * step : 2 * step + 2]
@@ -500,7 +504,7 @@
             for i, array in enumerate(operands)
         ]
         + [
-            pltpu.VMEM((near, 2 * ROWS, padded), F32),
+            pltpu.VMEM((padded // LANES, near * 2 * ROWS, LANES), F32),
             pltpu.VMEM((near * 2 * ROWS // LANES, points_count, LANES), BF16),
             pltpu.VMEM((group, 2 * ROWS, 2 * panels), BF16),
             pltpu.VMEM((group, ROWS, panels), F32),

time: 50.6 us -> 52.9 us (1.045)
  Pallas kernels: 47.6 us -> 49.9 us
    pallas_call x1, Pallas kernels: 47.6 us -> 49.9 us  [local(): pl.pallas_call(functools.partial(wall_kernel, cells, walls, points_count)...]
where the time goes in v4:
time: 52.9 us; the launch traced here: 52.7 us
  Pallas kernels  49.9 us (94%)
  matrix products  1.58 us (3%)
  between operations  0.68 us (1%)
  local copies, waits for them, and re-layouts  0.59 us (1%)
    pallas_call x1, Pallas kernels, local(): pl.pallas_call(functools.partial(wall_kernel, cells, walls, points_count)...  49.9 us
    dot_general x1, matrix products, local(): jnp.einsum('qs,asc->aqc', harmonic, shape_coef, preferred_element_type=F32)  1.58 us

profile of v4, /device:TPU:0, one launch (start us, length us, event | category | flops | bytes accessed | tf_op | source)
XLA Modules:
  0.0 52.7 jit_solution(7419087172127646051)
XLA Ops:
  0.6 0.0 copy-start
  0.6 0.0 copy-start.2
  0.7 49.9 %shard_map.167 = f32[2,384]{1,0:T(2,128)} custom-call(s32[1,64]{1,0:T(1,128)} %bitcast.12, bf16[3,289,256]{2,1,0:T(8,128)(2,1)} %refs_1_.1, bf16[289,640]{1,0:T(8,128)(2,1)} %constant.15.refs_2_, f32[2,384]{1,0:T(2,128)} %refs_3_.1, bf16[3,289,256]{2,1,0:T(8,128)(2,1)} %refs_4_.1, s32[1,64]{1,0:T(1,128)} %bitcast.10, s32[1,64]{1,0:T(1,128)} %bitcast.11, ...), custom_call_target="tpu_custom_call" | custom-call | tf_op jit(solution)/shard_map/pallas_call | solution.py:497
  50.5 0.0 copy-done
  50.5 0.0 copy-done.2
  50.5 0.0 copy-start.1
  50.5 1.6 %fusion = bf16[3,578,256]{2,1,0:T(8,128)(2,1)} fusion(bf16[578,289,1]{0,1,2:T(8,128)(2,1)S(1)} %copy-done.2, bf16[3,289,256]{2,1,0:T(8,128)(2,1)S(1)} %copy-done), kind=kOutput, calls=%fused_computation.1 | convolution fusion | flops 257020416 | bytes 1665796 | tf_op jit(solution)/shard_map/qs,asc->aqc/dot_general | solution.py:473
  52.1 0.0 copy-done.1
  52.1 0.6 %copy.19 = f32[2,384]{1,0:T(2,128)} copy(f32[2,384]{1,0:T(2,128)S(1)} %copy-done.1) | data formatting | bytes 6144
Async XLA Ops:
  0.6 49.9 %copy-start = (bf16[3,289,256]{2,1,0:T(8,128)(2,1)S(1)}, bf16[3,289,256]{2,1,0:T(8,128)(2,1)}, u32[]{:S(2)}) copy-start(bf16[3,289,256]{2,1,0:T(8,128)(2,1)} %refs_1_.1) | copy-start | bytes 1331716
  0.6 49.9 %copy-start.2 = (bf16[578,289,1]{0,1,2:T(8,128)(2,1)S(1)}, bf16[578,289,1]{0,1,2:T(8,128)(2,1)}, u32[]{:S(2)}) copy-start(bf16[578,289,1]{0,1,2:T(8,128)(2,1)} %constant.16) | copy-start | bytes 1002256
  50.5 1.6 %copy-start.1 = (f32[2,384]{1,0:T(2,128)S(1)}, f32[2,384]{1,0:T(2,128)}, u32[]{:S(2)}) copy-start(f32[2,384]{1,0:T(2,128)} %shard_map.167) | copy-start | bytes 9220

commit v5 on v3

--- a/solution.py
+++ b/solution.py
@@ -222,7 +222,7 @@
 
     each(walls - 1, lambda i: center_copy(i + 1).start())
 
-    for load in loads[4:]:
+    for load in loads[4:11]:
         load.wait()
     picked = jnp.concatenate(picked + pick(force_ref), axis=0)
     grid = rounded(jnp.dot(picked, harm_ref[...], preferred_element_type=F32))
@@ -313,10 +313,10 @@
             whole = jnp.dot(bt_sc[g], weights, preferred_element_type=F32)
             for start in range(0, points_count, SPAN):
                 stop = min(start + SPAN, points_count)
-                both = whole[start:stop]
+                both = whole[start:stop].astype(BF16)
                 inverse = lax.rsqrt(both[:, :panels])
                 along = both[:, panels:] * (inverse * inverse * inverse)
-                pair = jnp.concatenate([along.astype(BF16), inverse.astype(BF16)], axis=1)
+                pair = jnp.concatenate([along, inverse], axis=1)
                 total += jnp.dot(rows[:, start:stop], pair, preferred_element_type=F32)
             summed = total[:ROWS, :panels] + total[ROWS:, panels:]
             v_sc[pl.ds(pl.multiple_of(r * 8, 8), 8), :] = summed[:8] + summed[8:]
@@ -362,6 +362,8 @@
         low = jnp.broadcast_to(vector.astype(BF16), (ROWS, vector.shape[1]))
         return lax.dot_general(low, blocks_ref[t, b], NT, preferred_element_type=F32)[0:1]
 
+    for load in loads[11:]:
+        load.wait()
     density = rhs
     for step in range(ITERS):
         table_sc, nbr_sc = step_sc[2 * step : 2 * step + 2]

time: 50.6 us -> 50.6 us (level)
  no operation moved by 1% of the time
where the time goes in v5:
time: 50.6 us; the launch traced here: 50.4 us
  Pallas kernels  47.6 us (94%)
  matrix products  1.58 us (3%)
  between operations  0.68 us (1%)
  local copies, waits for them, and re-layouts  0.59 us (1%)
    pallas_call x1, Pallas kernels, local(): pl.pallas_call(functools.partial(wall_kernel, cells, walls, points_count)...  47.6 us
    dot_general x1, matrix products, local(): jnp.einsum('qs,asc->aqc', harmonic, shape_coef, preferred_element_type=F32)  1.58 us

profile of v5, /device:TPU:0, one launch (start us, length us, event | category | flops | bytes accessed | tf_op | source)
XLA Modules:
  0.0 50.4 jit_solution(10075779721958107294)
XLA Ops:
  0.6 0.0 copy-start
  0.6 0.0 copy-start.2
  0.7 47.6 %shard_map.167 = f32[2,384]{1,0:T(2,128)} custom-call(s32[1,64]{1,0:T(1,128)} %bitcast.12, bf16[3,289,256]{2,1,0:T(8,128)(2,1)} %refs_1_.1, bf16[289,640]{1,0:T(8,128)(2,1)} %constant.15.refs_2_, f32[2,384]{1,0:T(2,128)} %refs_3_.1, bf16[3,289,256]{2,1,0:T(8,128)(2,1)} %refs_4_.1, s32[1,64]{1,0:T(1,128)} %bitcast.10, s32[1,64]{1,0:T(1,128)} %bitcast.11, ...), custom_call_target="tpu_custom_call" | custom-call | tf_op jit(solution)/shard_map/pallas_call | solution.py:495
  48.3 0.0 copy-done
  48.3 0.0 copy-done.2
  48.3 0.0 copy-start.1
  48.3 1.6 %fusion = bf16[3,578,256]{2,1,0:T(8,128)(2,1)} fusion(bf16[578,289,1]{0,1,2:T(8,128)(2,1)S(1)} %copy-done.2, bf16[3,289,256]{2,1,0:T(8,128)(2,1)S(1)} %copy-done), kind=kOutput, calls=%fused_computation.1 | convolution fusion | flops 257020416 | bytes 1665796 | tf_op jit(solution)/shard_map/qs,asc->aqc/dot_general | solution.py:471
  49.9 0.0 copy-done.1
  49.9 0.6 %copy.19 = f32[2,384]{1,0:T(2,128)} copy(f32[2,384]{1,0:T(2,128)S(1)} %copy-done.1) | data formatting | bytes 6144
Async XLA Ops:
  0.6 47.6 %copy-start = (bf16[3,289,256]{2,1,0:T(8,128)(2,1)S(1)}, bf16[3,289,256]{2,1,0:T(8,128)(2,1)}, u32[]{:S(2)}) copy-start(bf16[3,289,256]{2,1,0:T(8,128)(2,1)} %refs_1_.1) | copy-start | bytes 1331716
  0.6 47.6 %copy-start.2 = (bf16[578,289,1]{0,1,2:T(8,128)(2,1)S(1)}, bf16[578,289,1]{0,1,2:T(8,128)(2,1)}, u32[]{:S(2)}) copy-start(bf16[578,289,1]{0,1,2:T(8,128)(2,1)} %constant.16) | copy-start | bytes 1002256
  48.3 1.6 %copy-start.1 = (f32[2,384]{1,0:T(2,128)S(1)}, f32[2,384]{1,0:T(2,128)}, u32[]{:S(2)}) copy-start(f32[2,384]{1,0:T(2,128)} %shard_map.167) | copy-start | bytes 9220

commit v6 on v5

--- a/solution.py
+++ b/solution.py
@@ -72,6 +72,11 @@
 
 def rounded(value):
     return value.astype(BF16).astype(F32)
+
+
+def split2(value):
+    first = rounded(value)
+    return first, rounded(value - first)
 
 
 def split3(value):
@@ -228,8 +233,14 @@
     grid = rounded(jnp.dot(picked, harm_ref[...], preferred_element_type=F32))
     points = [grid[a * near : (a + 1) * near] for a in range(3)]
     forces = [grid[a * near : (a + 1) * near] for a in range(3, 6)]
-    zero = jnp.zeros_like(points[0])
-    one = zero + 1.0
+    part = lax.broadcasted_iota(jnp.int32, b_sc.shape[1:], 0)
+    fixed = jnp.where((part >= 3) & (part < 6), 1.0, 0.0)
+
+    def fill(r, carry):
+        b_sc[r] = fixed
+        return carry
+
+    lax.fori_loop(0, near, fill, 0, unroll=4)
     square = points[0] * points[0] + points[1] * points[1] + points[2] * points[2] + soft_core
     inner = points[0] * forces[0] + points[1] * forces[1] + points[2] * forces[2]
     for a in range(3):
@@ -238,14 +249,9 @@
             put(a, half, value)
             put(12 + a, half, value)
         put(8 + a, 0, points[a])
-        put(8 + a, 1, zero)
-        put(3 + a, 0, one)
-        put(3 + a, 1, zero)
-    for row, sq, inn in zip((6, 7, 15), split3(square), split3(inner)):
+    for row, sq, inn in zip((6, 7), split2(square), split2(inner)):
         put(row, 0, sq)
         put(row, 1, -inn)
-    put(11, 0, zero)
-    put(11, 1, zero)
 
     def turn(g, carry):
         for j in range(chunks):
@@ -303,26 +309,38 @@
 
     empty = jnp.zeros((2 * ROWS, 2 * panels), BF16)
 
-    def pair_rows(g, carry):
-        for i in range(batch):
-            r = g * batch + i
-            panel = a_sc[dest_s[r] * clusters + slot_s[r]]
-            weights = jnp.concatenate([panel if k == i else empty for k in range(batch)], axis=0)
-            rows = b_sc[r].astype(BF16)
-            total = jnp.zeros((2 * ROWS, 2 * panels), F32)
-            whole = jnp.dot(bt_sc[g], weights, preferred_element_type=F32)
-            for start in range(0, points_count, SPAN):
-                stop = min(start + SPAN, points_count)
-                both = whole[start:stop].astype(BF16)
-                inverse = lax.rsqrt(both[:, :panels])
-                along = both[:, panels:] * (inverse * inverse * inverse)
-                pair = jnp.concatenate([along, inverse], axis=1)
-                total += jnp.dot(rows[:, start:stop], pair, preferred_element_type=F32)
-            summed = total[:ROWS, :panels] + total[ROWS:, panels:]
-            v_sc[pl.ds(pl.multiple_of(r * 8, 8), 8), :] = summed[:8] + summed[8:]
+    def fields(g, i):
+        r = g * batch + i
+        panel = a_sc[dest_s[r] * clusters + slot_s[r]]
+        weights = jnp.concatenate([panel if k == i else empty for k in range(batch)], axis=0)
+        return jnp.dot(bt_sc[g], weights, preferred_element_type=F32)
+
+    def reduce_row(r, whole):
+        rows = b_sc[r].astype(BF16)
+        total = jnp.zeros((2 * ROWS, 2 * panels), F32)
+        for start in range(0, points_count, SPAN):
+            stop = min(start + SPAN, points_count)
+            both = whole[start:stop]
+            inverse = lax.rsqrt(both[:, :panels])
+            along = both[:, panels:] * (inverse * inverse * inverse)
+            pair = jnp.concatenate([along.astype(BF16), inverse.astype(BF16)], axis=1)
+            total += jnp.dot(rows[:, start:stop], pair, preferred_element_type=F32)
+        summed = total[:ROWS, :panels] + total[ROWS:, panels:]
+        v_sc[pl.ds(pl.multiple_of(r * 8, 8), 8), :] = summed[:8] + summed[8:]
+
+    joined = math.gcd(near // batch, 2)
+
+    def pair_rows(n, carry):
+        places = [(n * joined + k, i) for k in range(joined) for i in range(batch)]
+        ahead = fields(*places[0])
+        for at, (g, i) in enumerate(places):
+            whole = ahead
+            if at + 1 < len(places):
+                ahead = fields(*places[at + 1])
+            reduce_row(g * batch + i, whole)
         return carry
 
-    lax.fori_loop(0, near // batch, pair_rows, 0)
+    lax.fori_loop(0, near // batch // joined, pair_rows, 0)
 
     value = v_sc[...]
     high = value.astype(BF16)

time: 50.6 us -> 40.4 us (0.80)
  Pallas kernels: 47.6 us -> 37.4 us
    pallas_call x1, Pallas kernels: 47.6 us -> 37.4 us  [local(): pl.pallas_call(functools.partial(wall_kernel, cells, walls, points_count)...]
where the time goes in v6:
time: 40.4 us; the launch traced here: 40.3 us
  Pallas kernels  37.4 us (93%)
  matrix products  1.58 us (4%)
  between operations  0.68 us (2%)
  local copies, waits for them, and re-layouts  0.59 us (1%)
    pallas_call x1, Pallas kernels, local(): pl.pallas_call(functools.partial(wall_kernel, cells, walls, points_count)...  37.4 us
    dot_general x1, matrix products, local(): jnp.einsum('qs,asc->aqc', harmonic, shape_coef, preferred_element_type=F32)  1.58 us

profile of v6, /device:TPU:0, one launch (start us, length us, event | category | flops | bytes accessed | tf_op | source)
XLA Modules:
  0.0 40.3 jit_solution(15170806263450105575)
XLA Ops:
  0.6 0.0 copy-start
  0.6 0.0 copy-start.2
  0.7 37.4 %shard_map.167 = f32[2,384]{1,0:T(2,128)} custom-call(s32[1,64]{1,0:T(1,128)} %bitcast.12, bf16[3,289,256]{2,1,0:T(8,128)(2,1)} %refs_1_.1, bf16[289,640]{1,0:T(8,128)(2,1)} %constant.15.refs_2_, f32[2,384]{1,0:T(2,128)} %refs_3_.1, bf16[3,289,256]{2,1,0:T(8,128)(2,1)} %refs_4_.1, s32[1,64]{1,0:T(1,128)} %bitcast.10, s32[1,64]{1,0:T(1,128)} %bitcast.11, ...), custom_call_target="tpu_custom_call" | custom-call | tf_op jit(solution)/shard_map/pallas_call | solution.py:513
  38.1 0.0 copy-done
  38.1 0.0 copy-done.2
  38.1 0.0 copy-start.1
  38.1 1.6 %fusion = bf16[3,578,256]{2,1,0:T(8,128)(2,1)} fusion(bf16[578,289,1]{0,1,2:T(8,128)(2,1)S(1)} %copy-done.2, bf16[3,289,256]{2,1,0:T(8,128)(2,1)S(1)} %copy-done), kind=kOutput, calls=%fused_computation.1 | convolution fusion | flops 257020416 | bytes 1665796 | tf_op jit(solution)/shard_map/qs,asc->aqc/dot_general | solution.py:489
  39.7 0.0 copy-done.1
  39.7 0.6 %copy.19 = f32[2,384]{1,0:T(2,128)} copy(f32[2,384]{1,0:T(2,128)S(1)} %copy-done.1) | data formatting | bytes 6144
Async XLA Ops:
  0.6 37.5 %copy-start = (bf16[3,289,256]{2,1,0:T(8,128)(2,1)S(1)}, bf16[3,289,256]{2,1,0:T(8,128)(2,1)}, u32[]{:S(2)}) copy-start(bf16[3,289,256]{2,1,0:T(8,128)(2,1)} %refs_1_.1) | copy-start | bytes 1331716
  0.6 37.5 %copy-start.2 = (bf16[578,289,1]{0,1,2:T(8,128)(2,1)S(1)}, bf16[578,289,1]{0,1,2:T(8,128)(2,1)}, u32[]{:S(2)}) copy-start(bf16[578,289,1]{0,1,2:T(8,128)(2,1)} %constant.16) | copy-start | bytes 1002256
  38.1 1.6 %copy-start.1 = (f32[2,384]{1,0:T(2,128)S(1)}, f32[2,384]{1,0:T(2,128)}, u32[]{:S(2)}) copy-start(f32[2,384]{1,0:T(2,128)} %shard_map.167) | copy-start | bytes 9220
